TPU v7x, 32 devices: a whole 2x2x4 slice. The times are simulated.
32 devices in a mesh: row: 4 (over y, x), col: 8 (over z, core).
Axes of the slice: x: 2, y: 2, z: 4, core: 2. Of those that a mesh axis runs over, the one named last changes fastest.
Arguments:
- a_blocks: bfloat16 [8, 4, 16, 32, 128], P('col', 'row'), may hold values from -1 to 1
- a_scale: float32 [8, 4, 16, 4], P('col', 'row'), may hold values from 0.25 to 4
- a_cols: int32 [8, 4, 16, 4], P('col', 'row'), may hold values from 0 to 1023, as said below
- b_blocks: bfloat16 [8, 4, 1024, 32, 128], P('col', 'row'), may hold values from -1 to 1
- b_scale: float32 [8, 4, 1024, 4], P('col', 'row'), may hold values from 0.25 to 4
- b_cols: int32 [8, 4, 1024, 4], P('col', 'row'), may hold values from 0 to 511, as said below
Outputs:
- product: bfloat16 [8, 4, 8, 32, 16384], P('col', 'row')
Inputs may be any that keep to these rules, and one draw needn't show every extreme that they name: `a_cols`: the 4 columns of each block row are distinct. `b_cols`: the 4 columns of each block row are distinct.
All inputs are finite; a program needn't handle non-finite values.
Results may differ from a plain program's by a relative error of at most 0.0034.
Values may be sent and summed in bfloat16 or wider, within the bound.
No kernel may reach another device: no remote copies, remote signals or barrier semaphores. Data moves between devices by JAX's collectives and lax.ppermute only.
A program may use at most 192 MiB of HBM per device.

v0:
```python
import functools

import jax
import jax.numpy as jnp
from jax import lax
from jax.experimental import pallas as pl
from jax.experimental.pallas import tpu as pltpu
from jax.sharding import PartitionSpec as P

JW = 512
LANES = 128
META = 16
PARTS = 5
CHUNKS = 4
F32, BF16, I32 = jnp.float32, jnp.bfloat16, jnp.int32
VMEM_LIMIT = 12 * 1024 * 1024


def three_parts(x):
    high = x.astype(BF16).astype(F32)
    rest = x - high
    mid = rest.astype(BF16).astype(F32)
    return [high, mid, (rest - mid).astype(BF16).astype(F32)]


def stacked(parts, rows):
    which = lax.broadcasted_iota(I32, (rows, parts[0].shape[1]), 0)
    tile = jnp.zeros(which.shape, F32)
    for at, part in enumerate(parts):
        tile = jnp.where(which == at, jnp.broadcast_to(part, which.shape), tile)
    return tile


def entries(values, first, half, rb):
    ra = values.shape[0]
    one = [values[m : m + 1, first : first + half] for m in range(ra)]
    return jnp.concatenate(one * rb, axis=1)


class Sizes:
    def __init__(self, half, ra, rb, bs):
        self.half, self.ra, self.rb, self.bs = half, ra, rb, bs
        self.wide = ra * bs
        self.tiles = JW * bs // LANES

    def message(self, rows):
        return pltpu.VMEM(((rows[1] - rows[0]) * self.wide + META, self.rb * self.bs), BF16)

    def window(self):
        return pltpu.VMEM((self.half, self.tiles, self.bs, LANES), F32)


def kernel_call(name, body, ins, outs, aliases=(), scratch=None):
    scratch = scratch or {}
    names = list(ins) + list(outs) + list(scratch)

    def kernel(*refs):
        body(dict(zip(names, refs)))

    args, in_specs = [], []
    for array, place in ins.values():
        if place == "smem":
            spec = pl.BlockSpec(memory_space=pltpu.SMEM)
        elif place == "vmem":
            spec = pl.BlockSpec(memory_space=pltpu.VMEM)
            array = pltpu.with_memory_space_constraint(array, pltpu.VMEM)
        elif place == "hbm":
            spec = pl.BlockSpec(memory_space=pltpu.HBM)
            array = pltpu.with_memory_space_constraint(array, pltpu.HBM)
        else:
            spec = pl.BlockSpec(memory_space=pl.ANY)
        args.append(array)
        in_specs.append(spec)
    out_specs = [
        pl.BlockSpec(memory_space=pl.ANY if isinstance(shape, jax.ShapeDtypeStruct) else pltpu.VMEM)
        for shape in outs.values()
    ]
    got = pl.pallas_call(
        kernel,
        out_shape=list(outs.values()),
        in_specs=in_specs,
        out_specs=out_specs,
        input_output_aliases={list(ins).index(a): list(outs).index(b) for a, b in aliases},
        scratch_shapes=list(scratch.values()),
        compiler_params=pltpu.CompilerParams(vmem_limit_bytes=VMEM_LIMIT),
        cost_estimate=pl.CostEstimate(flops=FLOPS, bytes_accessed=1024, transcendentals=0),
        name=name,
    )(*args)
    return dict(zip(outs, got))


FLOPS = 0


class Gather:
    def __init__(self, sizes, refs, out, flip, rows, cols, sem):
        self.z, self.refs, self.out, self.flip, self.rows, self.cols = sizes, refs, refs[out], flip, rows, cols
        self.sem = sem

    def start(self):
        z, refs = self.z, self.refs
        cols, b = refs[self.cols + "_s"], refs["b"]
        base = (refs["info"][0] ^ self.flip) * z.half
        first, last = self.rows

        def one_row(i, _):
            for m in range(z.ra):
                at = pl.multiple_of(((i - first) * z.ra + m) * z.bs, z.bs)
                source = b.at[cols[m, base + i]]
                pltpu.make_async_copy(source, self.out.at[pl.ds(at, z.bs)], self.sem).start()
            return 0

        lax.fori_loop(first, last, one_row, 0, unroll=2)

    def finish(self):
        z, refs = self.z, self.refs
        table, cols = refs["table"], refs[self.cols + "_v"][...]
        kw = table.shape[1]
        both = [entries(cols, h * z.half, z.half, z.rb) for h in range(2)]
        odd = (refs["info"][0] ^ self.flip) == 1
        named = jnp.where(odd, both[1], both[0])
        named = jnp.broadcast_to(named, (kw, named.shape[1]))
        picked = lax.broadcasted_iota(I32, named.shape, 0) == named
        picked = jnp.where(picked, 1.0, 0.0).astype(BF16)
        found = jnp.dot(table[...], picked, preferred_element_type=F32)
        slot = lax.broadcasted_iota(I32, (1, found.shape[1]), 1) // (z.ra * z.half)
        parts = []
        for part in range(PARTS):
            value = found[part * z.rb : part * z.rb + 1]
            for n in range(1, z.rb):
                value = jnp.where(slot == n, found[part * z.rb + n : part * z.rb + n + 1], value)
            parts.append(value)
        size = (self.rows[1] - self.rows[0]) * z.wide
        self.out[pl.ds(size, META), :] = stacked(parts, META).astype(BF16)
        blocks = self.out.at[pl.ds(0, size)]
        pltpu.make_async_copy(blocks, blocks, self.sem).wait()


class Add:
    def __init__(self, sizes, refs, a, b, rows):
        self.z, self.refs, self.a, self.b, self.rows = sizes, refs, a, b, rows

    @staticmethod
    def scratch(sizes, rows):
        return {
            "prod": pltpu.VMEM(((rows[1] - rows[0]) * sizes.wide, LANES), F32),
            "scl_v": pltpu.VMEM((8, LANES), F32),
            "col_v": pltpu.VMEM((8, LANES), I32),
            "scl_s": pltpu.SMEM((8, LANES), F32),
            "col_s": pltpu.SMEM((8, LANES), I32),
            "add_sems": pltpu.SemaphoreType.DMA((2,)),
        }

    def start(self):
        z, refs, a, b = self.z, self.refs, self.a, self.b
        first, last = self.rows
        scl_v, col_v = refs["scl_v"], refs["col_v"]
        a_meta = a[pl.ds(a.shape[0] - META, META), :].astype(F32)
        b_meta = b[pl.ds(b.shape[0] - META, META), :].astype(F32)
        scl_a = a_meta[0:1] + a_meta[1:2] + a_meta[2:3]
        scl_b = b_meta[0:1] + b_meta[1:2] + b_meta[2:3]
        scl_v[...] = jnp.broadcast_to(scl_a * scl_b, scl_v.shape)
        col_v[...] = jnp.broadcast_to((b_meta[3:4] * 256.0 + b_meta[4:5]).astype(I32), col_v.shape)
        sems = refs["add_sems"]
        self.moves = [
            pltpu.make_async_copy(scl_v, refs["scl_s"], sems.at[0]),
            pltpu.make_async_copy(col_v, refs["col_s"], sems.at[1]),
        ]
        for move in self.moves:
            move.start()
        row_block = lax.broadcasted_iota(I32, (z.wide, z.wide), 0) // z.bs
        col_block = lax.broadcasted_iota(I32, (z.wide, z.wide), 1) // z.bs
        diagonal = jnp.where(row_block == col_block, 1.0, 0.0).astype(BF16)
        for i in range(first, last):
            left = a[pl.ds(i * z.bs, z.bs), :]
            left = jnp.concatenate([left] * z.ra, axis=0) * diagonal
            rows = pl.ds((i - first) * z.wide, z.wide)
            refs["prod"][rows, :] = jnp.dot(left, b[rows, :], preferred_element_type=F32)

    def finish(self):
        z, refs = self.z, self.refs
        first, last = self.rows
        acc, prod, scl_s, col_s = refs["acc"], refs["prod"], refs["scl_s"], refs["col_s"]
        per = LANES // z.bs
        for move in self.moves:
            move.wait()
        lane_block = lax.broadcasted_iota(I32, (z.bs, LANES), 1) // z.bs

        def one_row(i, _):
            for m in range(z.ra):
                value = prod[pl.ds(pl.multiple_of(((i - first) * z.ra + m) * z.bs, z.bs), z.bs), :]
                placed = []
                for n in range(z.rb):
                    entry = (n * z.ra + m) * z.half + i
                    column = col_s[0, entry]
                    place = column & (per - 1)
                    moved = pltpu.roll(value, ((place - n) & (per - 1)) * z.bs, 1)
                    moved = jnp.where(lane_block == place, moved * scl_s[0, entry], 0.0)
                    placed.append((column // per, moved))
                for tile, moved in placed:
                    acc[i, tile] = acc[i, tile] + moved
            return 0

        lax.fori_loop(first, last, one_row, 0)


def clear(acc):
    for i in range(acc.shape[0]):

        def clear_tile(tile, _, i=i):
            acc[i, tile] = jnp.zeros(acc.shape[2:], F32)
            return 0

        lax.fori_loop(0, acc.shape[1], clear_tile, 0, unroll=8)


def write_out(sizes, refs, rows):
    acc, stage, sems, out = refs["acc"], refs["stage"], refs["out_sems"], refs["out"]
    slots = stage.shape[0]
    tiles = sizes.tiles // CHUNKS
    pieces = [(i, chunk) for i in range(*rows) for chunk in range(CHUNKS)]

    def send(at):
        i, chunk = pieces[at]
        columns = pl.ds(chunk * tiles * LANES, tiles * LANES)
        return pltpu.make_async_copy(stage.at[at % slots], out.at[i, :, columns], sems.at[at % slots])

    for at, (i, chunk) in enumerate(pieces):
        if at >= slots:
            send(at - slots).wait()
        for tile in range(tiles):
            stage[at % slots, :, pl.ds(tile * LANES, LANES)] = acc[i, chunk * tiles + tile].astype(BF16)
        send(at).start()
    for at in range(max(0, len(pieces) - slots), len(pieces)):
        send(at).wait()


def first_answer(z, info, cols, own_cols, b_scl, b_pos, b, rows):
    rb, kw = b_scl.shape

    def body(refs):
        answer = Gather(z, refs, "message", 0, rows, "cols", refs["sems"].at[0])
        moves = [
            pltpu.make_async_copy(refs["b_scl"], refs["scl"], refs["sems"].at[1]),
            pltpu.make_async_copy(refs["b_pos"], refs["pos"], refs["sems"].at[2]),
        ]
        for move in moves:
            move.start()
        answer.start()
        refs["own"][...] = refs["own_cols"][...]
        for move in moves:
            move.wait()
        scale, column = refs["scl"][...], refs["pos"][...]
        table = three_parts(scale) + [(column >> 8).astype(F32), (column & 255).astype(F32)]
        table.append(jnp.zeros((refs["table"].shape[0] - PARTS * rb, kw), F32))
        refs["table"][...] = jnp.concatenate(table, axis=0).astype(BF16)
        answer.finish()

    return kernel_call(
        "first_answer",
        body,
        {
            "info": (info, "smem"),
            "cols_s": (cols, "smem"),
            "cols_v": (cols, "vmem"),
            "own_cols": (own_cols, "vmem"),
            "b_scl": (b_scl, "hbm"),
            "b_pos": (b_pos, "hbm"),
            "b": (b, "hbm"),
        },
        {
            "table": pltpu.VMEM((-(-PARTS * rb // 16) * 16, kw), BF16),
            "message": z.message(rows),
            "own": pltpu.VMEM(own_cols.shape, I32),
        },
        scratch={
            "scl": pltpu.VMEM(b_scl.shape, F32),
            "pos": pltpu.VMEM(b_pos.shape, I32),
            "sems": pltpu.SemaphoreType.DMA((3,)),
        },
    )


def second_answer(z, info, cols, table, b, rows, a, a_scl, panels):
    def body(refs):
        answer = Gather(z, refs, "message", 1, rows, "cols", refs["sems"].at[0])
        answer.start()
        scale = refs["a_scl"][...]
        size = z.half * z.bs
        spread = refs["spread"]
        for side in range(2):
            blocks = refs["a"][pl.ds(side * size, size), :]
            scales = stacked(three_parts(entries(scale, side * z.half, z.half, z.rb)), META).astype(BF16)
            for panel in range(panels):
                spread[2 * panel + side, pl.ds(0, size), :] = blocks
                spread[2 * panel + side, pl.ds(size, META), :] = scales
        answer.finish()

    return kernel_call(
        "second_answer",
        body,
        {
            "info": (info, "smem"),
            "cols_s": (cols, "smem"),
            "cols_v": (cols, "vmem"),
            "table": (table, "vmem"),
            "b": (b, "hbm"),
            "a": (a, "vmem"),
            "a_scl": (a_scl, "vmem"),
        },
        {
            "message": z.message(rows),
            "spread": pltpu.VMEM((2 * panels, z.half * z.bs + META, z.wide), BF16),
        },
        scratch={"sems": pltpu.SemaphoreType.DMA((1,))},
    )


def own_blocks(z, info, cols, table, b, rows, left, acc):
    def body(refs):
        answer = Gather(z, refs, "message", 1, rows, "cols", refs["sems"].at[0])
        local = Gather(z, refs, "local", 0, rows, "cols", refs["sems"].at[1])
        local.start()
        answer.start()
        local.finish()
        add = Add(z, refs, refs["left"].at[refs["info"][1]], refs["local"], rows)
        add.start()
        answer.finish()
        add.finish()

    return kernel_call(
        "own_blocks",
        body,
        {
            "info": (info, "smem"),
            "cols_s": (cols, "smem"),
            "cols_v": (cols, "vmem"),
            "table": (table, "vmem"),
            "b": (b, "hbm"),
            "left": (left, "vmem"),
            "acc_in": (acc, "vmem"),
        },
        {"acc": z.window(), "message": z.message(rows)},
        aliases=[("acc_in", "acc")],
        scratch={
            "sems": pltpu.SemaphoreType.DMA((2,)),
            "local": z.message(rows),
            **Add.scratch(z, rows),
        },
    )


def add_message(z, info, left, by, flip, message, rows, acc, answers=(), table=None, b=None, write=False, out=None):
    ins = {
        "info": (info, "smem"),
        "left": (left, "vmem"),
        "arrived": (message, "vmem"),
    }
    outs = {"acc": z.window()}
    aliases = []
    if acc is not None:
        ins["acc_in"] = (acc, "vmem")
        aliases.append(("acc_in", "acc"))
    scratch = Add.scratch(z, rows)
    if answers:
        ins.update(table=(table, "vmem"), b=(b, "hbm"))
        scratch["sems"] = pltpu.SemaphoreType.DMA((len(answers),))
    for at, (cols, _, span) in enumerate(answers):
        ins[f"cols{at}_s"] = (cols, "smem")
        ins[f"cols{at}_v"] = (cols, "vmem")
        outs[f"message{at}"] = z.message(span)
    if write:
        outs["out"] = jax.ShapeDtypeStruct((z.half, z.bs, JW * z.bs), BF16)
        scratch["stage"] = pltpu.VMEM((8, z.bs, JW * z.bs // CHUNKS), BF16)
        scratch["out_sems"] = pltpu.SemaphoreType.DMA((8,))
        if out is not None:
            ins["out_in"] = (out, "any")
            aliases.append(("out_in", "out"))

    def body(refs):
        gathers = [
            Gather(z, refs, f"message{at}", side, span, f"cols{at}", refs["sems"].at[at])
            for at, (_, side, span) in enumerate(answers)
        ]
        for gather in gathers:
            gather.start()
        place = refs["info"][1 + 2 * by + flip]
        add = Add(z, refs, refs["left"].at[place], refs["arrived"], rows)
        add.start()
        if acc is None:
            clear(refs["acc"])
        for gather in gathers:
            gather.finish()
        add.finish()
        if write:
            write_out(z, refs, rows)

    got = kernel_call("add_message", body, ins, outs, aliases, scratch)
    return got["acc"], [got[f"message{at}"] for at in range(len(answers))], got.get("out")


def on_device(a_blocks, a_scale, a_cols, b_blocks, b_scale, b_cols):
    panels = lax.axis_size("row")
    columns = lax.axis_size("col")
    halves = columns // panels
    a_part, a_scl, a_pos = a_blocks[0, 0], a_scale[0, 0].T, a_cols[0, 0].T
    b_part = b_blocks[0, 0]
    b_scl, b_pos = b_scale[0, 0].T, b_cols[0, 0].T
    nrows, bs, _ = a_part.shape
    half = nrows // halves
    z = Sizes(half, a_scl.shape[0], b_scl.shape[0], bs)
    row = lax.axis_index("row")
    parity = lax.axis_index("col") % halves
    places = [(row - by) % panels * halves + (parity ^ flip) for by in range(panels) for flip in range(halves)]
    info = jnp.stack([parity] + places).astype(I32)

    def step(value, by, flip):
        pairs = [
            (c, ((c // halves + by) % panels) * halves + (c % halves ^ flip)) for c in range(columns)
        ]
        return lax.ppermute(value, "col", pairs)

    def named_by(by, cols):
        pairs = []
        for r in range(panels):
            for c in range(columns):
                to_row = (r + by) % panels
                to_col = (c - halves * by) % columns
                pairs.append((r * columns + c, to_row * columns + to_col))
        return lax.ppermute(cols, ("row", "col"), pairs)

    order = sorted(range(1, panels), key=lambda by: -min(by, panels - by))
    every = (0, half)
    early = (0, half - max(1, half // 4))
    late = (early[1], half)
    queue = [(by, flip, every) for by in order for flip in range(halves)]
    queue[-1:] = [(order[-1], 1, early), (order[-1], 1, late)]

    asked = {order[0]: named_by(order[0], a_pos)}
    got = first_answer(z, info, asked[order[0]], a_pos, b_scl, b_pos, b_part, every)
    table, own_cols = got["table"], got["own"]
    moving = [step(got["message"], order[0], 0)]
    for by in order[1:]:
        asked[by] = named_by(by, own_cols)
    a_flat = a_part.reshape(nrows * bs, z.wide)
    got = second_answer(z, info, asked[order[0]], table, b_part, every, a_flat, a_scl, panels)
    moving.append(step(got["message"], order[0], 1))

    groups = [
        [r * columns + c for r in range(panels) for c in range(s * halves, (s + 1) * halves)]
        for s in range(panels)
    ]
    left = lax.all_to_all(got["spread"], ("row", "col"), 0, 0, axis_index_groups=groups)

    acc = None
    taken = None
    out = None
    for at, (by, flip, rows) in enumerate(queue):
        upto = min(len(queue), at + (3 if at == 0 else 4))
        if upto == len(queue) - 1:
            upto = len(queue)
        later = queue[len(moving) : upto]
        if at == len(queue) - 2:
            acc = add_message(z, info, left, 0, 1, taken, every, acc)[0]
        write = at >= len(queue) - 2
        acc, answers, out = add_message(
            z, info, left, by, flip, moving[at], rows, acc,
            answers=[(asked[to], side, span) for to, side, span in later],
            table=table, b=b_part, write=write, out=out,
        )
        for answer, (to, side, _) in zip(answers, later):
            moving.append(step(answer, to, side))
        if at == 0:
            mine = own_blocks(z, info, own_cols, table, b_part, every, left, acc)
            acc = mine["acc"]
            taken = step(mine["message"], 0, 1)
    return out[None, None]


def solution(mesh):
    in_specs = (
        P("col", "row", None, None, None),
        P("col", "row", None, None),
        P("col", "row", None, None),
        P("col", "row", None, None, None),
        P("col", "row", None, None),
        P("col", "row", None, None),
    )
    out_specs = P("col", "row", None, None, None)
    return jax.shard_map(
        on_device, mesh=mesh, in_specs=in_specs, out_specs=out_specs, check_vma=False
    )
```

profile of v0, /device:TPU:19, one launch (start us, length us, event | category | flops | bytes accessed | tf_op | source)
XLA Modules:
  0.0 93.0 jit_solution(12832675482330788783)
XLA Ops:
  0.0 1.0 %collective-permute-start = (s32[4,16]{1,0:T(4,128)}, s32[4,16]{1,0:T(4,128)S(1)}, u32[]{:S(2)}, u32[]{:S(2)}) collective-permute-start(s32[4,16]{1,0:T(4,128)} %bitcast.25), channel_id=1, source_target_pairs={{0,20},{1,21},{2,22},{3,23},{4,16},{5,17},{6,18},{7,19},{8,28},{9,... | collective-permute-start | bytes 776 | tf_op jit(solution)/shard_map/ppermute | solution.py:430
  1.0 0.1 stack.39.refs_0_
  1.1 3.3 %collective-permute-done.refs_1_.refs_2_ = s32[4,16]{1,0:T(4,128)S(1)} collective-permute-done((s32[4,16]{1,0:T(4,128)}, s32[4,16]{1,0:T(4,128)S(1)}, u32[]{:S(2)}, u32[]{:S(2)}) %collective-permute-start) | collective-permute-done | bytes 288 | tf_op jit(solution)/shard_map/ppermute | solution.py:430
  4.4 0.0 copy-start.1
  4.4 0.7 copy-done.1
  5.1 1.6 %first_answer.1 = (bf16[32,1024]{1,0:T(8,128)(2,1)S(1)}, bf16[1040,128]{1,0:T(8,128)(2,1)S(1)}, s32[4,16]{1,0:T(4,128)S(1)}) custom-call(s32[9]{0:T(128)S(1)} %stack.39.refs_0_, s32[4,16]{1,0:T(4,128)S(1)} %collective-permute-done.refs_1_.refs_2_, s32[4,16]{1,0:T(4,128)S(1)} %collective-permute-done.refs_1_.refs_2_, s32[4,16]{1,0:T(4,128)S(1)} %bitcast.26, ...), custom_call_target="tpu_custom_call" | custom-call | bytes 1024 | tf_op jit(solution)/shard_map/first_answer/pallas_call | solution.py:78
  6.7 0.0 copy-start
  6.8 0.9 copy-done
  7.6 0.0 copy-start.2
  7.7 0.7 copy-done.2
  8.3 2.3 %second_answer.1 = (bf16[1040,128]{1,0:T(8,128)(2,1)S(1)}, bf16[8,272,128]{2,1,0:T(8,128)(2,1)}) custom-call(s32[9]{0:T(128)S(1)} %stack.39.refs_0_, s32[4,16]{1,0:T(4,128)S(1)} %collective-permute-done.refs_1_.refs_2_, s32[4,16]{1,0:T(4,128)S(1)} %collective-permute-done.refs_1_.refs_2_, bf16[32,1024]{1,0:T(8,128)(2,1)S(1)} %get-tuple-element.23.refs_3_.refs_4_, ...), custom_call_target="tpu_custom_call" | custom-call | bytes 1024 | tf_op jit(solution)/shard_map/second_answer/pallas_call | solution.py:78
  10.7 5.7 %all-to-all-start = ((bf16[8,272,128]{2,1,0:T(8,128)(2,1)}), bf16[8,272,128]{2,1,0:T(8,128)(2,1)S(1)}, u32[]{:S(2)}, u32[]{:S(2)}) async-start(bf16[8,272,128]{2,1,0:T(8,128)(2,1)} %get-tuple-element.24), calls=%async_computation | async-start | bytes 1114112 | tf_op jit(solution)/shard_map/all_to_all | solution.py:453
  16.4 0.1 collective-permute-start.1
  16.5 2.8 %collective-permute-start.4 = (bf16[1040,128]{1,0:T(8,128)(2,1)S(1)}, bf16[1040,128]{1,0:T(8,128)(2,1)S(1)}, u32[]{:S(2)}, u32[]{:S(2)}) collective-permute-start(bf16[1040,128]{1,0:T(8,128)(2,1)S(1)} %get-tuple-element.28), channel_id=1, source_target_pairs={{0,5},{1,4},{2,7},{3,6},{4,1},{5,0},{6,3},{7,2},{8,13},{9,12},{10,... | collective-permute-start | bytes 798728 | tf_op jit(solution)/shard_map/ppermute | solution.py:421
  19.3 1.1 %collective-permute-start.2 = (s32[4,16]{1,0:T(4,128)S(1)}, s32[4,16]{1,0:T(4,128)S(1)}, u32[]{:S(2)}, u32[]{:S(2)}) collective-permute-start(s32[4,16]{1,0:T(4,128)S(1)} %get-tuple-element.26.refs_1_.refs_2_), channel_id=1, source_target_pairs={{0,14},{1,15},{2,8},{3,9},{4,10},{5,11},{6,12},{7,13},{8,22},{9,23... | collective-permute-start | bytes 776 | tf_op jit(solution)/shard_map/ppermute | solution.py:430
  20.4 18.7 %collective-permute-done.2.refs_5_.refs_6_.refs_7_ = s32[4,16]{1,0:T(4,128)S(1)} collective-permute-done((s32[4,16]{1,0:T(4,128)S(1)}, s32[4,16]{1,0:T(4,128)S(1)}, u32[]{:S(2)}, u32[]{:S(2)}) %collective-permute-start.2) | collective-permute-done | bytes 288 | tf_op jit(solution)/shard_map/ppermute | solution.py:430
  39.0 0.0 collective-permute-done.1.refs_2_
  39.0 0.0 all-to-all-done.refs_1_.refs_5_
  39.0 3.8 %add_message.8 = (f32[8,128,32,128]{3,2,1,0:T(8,128)S(1)}, bf16[1040,128]{1,0:T(8,128)(2,1)S(1)}) custom-call(s32[9]{0:T(128)S(1)} %stack.39.refs_0_, bf16[8,272,128]{2,1,0:T(8,128)(2,1)S(1)} %all-to-all-done.refs_1_.refs_5_, bf16[1040,128]{1,0:T(8,128)(2,1)S(1)} %collective-permute-done.1.refs_2_, bf16[32,1024]{1,0:T(8,128)(2,1)S(1)} %get-tuple-element.23.refs_3_.refs_4_, ...), custom_call_target="tpu_custom_call" | custom-call | bytes 1024 | tf_op jit(solution)/shard_map/add_message/pallas_call | solution.py:78
  42.9 0.1 collective-permute-start.3
  43.0 0.1 collective-permute-start.5
  43.0 3.8 %own_blocks.1 = (f32[8,128,32,128]{3,2,1,0:T(8,128)S(1)}, bf16[1040,128]{1,0:T(8,128)(2,1)S(1)}) custom-call(s32[9]{0:T(128)S(1)} %stack.39.refs_0_, s32[4,16]{1,0:T(4,128)S(1)} %get-tuple-element.26.refs_1_.refs_2_, s32[4,16]{1,0:T(4,128)S(1)} %get-tuple-element.26.refs_1_.refs_2_, ...), custom_call_target="tpu_custom_call", output_to_operand_aliasing={{0}: (6, {})} | custom-call | bytes 1024 | tf_op jit(solution)/shard_map/own_blocks/pallas_call | solution.py:78
  46.8 4.8 %collective-permute-done.5.refs_8_.refs_9_.refs_6_.refs_7_ = s32[4,16]{1,0:T(4,128)S(1)} collective-permute-done((s32[4,16]{1,0:T(4,128)S(1)}, s32[4,16]{1,0:T(4,128)S(1)}, u32[]{:S(2)}, u32[]{:S(2)}) %collective-permute-start.5) | collective-permute-done | bytes 288 | tf_op jit(solution)/shard_map/ppermute | solution.py:430
  51.6 0.0 collective-permute-done.4.refs_2_
  51.6 3.2 %add_message.9 = (f32[8,128,32,128]{3,2,1,0:T(8,128)S(1)}, bf16[1040,128]{1,0:T(8,128)(2,1)S(1)}, bf16[1040,128]{1,0:T(8,128)(2,1)S(1)}) custom-call(s32[9]{0:T(128)S(1)} %stack.39.refs_0_, bf16[8,272,128]{2,1,0:T(8,128)(2,1)S(1)} %all-to-all-done.refs_1_.refs_5_, ...), custom_call_target="tpu_custom_call", output_to_operand_aliasing={{0}: (3, {})} | custom-call | bytes 1024 | tf_op jit(solution)/shard_map/add_message/pallas_call | solution.py:78
  54.9 3.2 %collective-permute-start.10 = (bf16[1040,128]{1,0:T(8,128)(2,1)S(1)}, bf16[1040,128]{1,0:T(8,128)(2,1)S(1)}, u32[]{:S(2)}, u32[]{:S(2)}) collective-permute-start(bf16[1040,128]{1,0:T(8,128)(2,1)S(1)} %get-tuple-element.36), channel_id=1, source_target_pairs={{0,3},{1,2},{2,5},{3,4},{4,7},{5,6},{6,1},{7,0},{8,11},{9,10},{10,... | collective-permute-start | bytes 798728 | tf_op jit(solution)/shard_map/ppermute | solution.py:421
  58.1 0.6 collective-permute-start.9
  58.7 0.5 collective-permute-start.8
  59.1 0.0 collective-permute-done.3.refs_2_
  59.2 3.2 %add_message.10 = (f32[8,128,32,128]{3,2,1,0:T(8,128)S(1)}, bf16[784,128]{1,0:T(8,128)(2,1)S(1)}, bf16[272,128]{1,0:T(8,128)(2,1)S(1)}) custom-call(s32[9]{0:T(128)S(1)} %stack.39.refs_0_, bf16[8,272,128]{2,1,0:T(8,128)(2,1)S(1)} %all-to-all-done.refs_1_.refs_5_, ...), custom_call_target="tpu_custom_call", output_to_operand_aliasing={{0}: (3, {})} | custom-call | bytes 1024 | tf_op jit(solution)/shard_map/add_message/pallas_call | solution.py:78
  62.4 1.5 %collective-permute-start.7 = (bf16[784,128]{1,0:T(8,128)(2,1)S(1)}, bf16[784,128]{1,0:T(8,128)(2,1)S(1)}, u32[]{:S(2)}, u32[]{:S(2)}) collective-permute-start(bf16[784,128]{1,0:T(8,128)(2,1)S(1)} %get-tuple-element.33), channel_id=1, source_target_pairs={{0,7},{1,6},{2,1},{3,0},{4,3},{5,2},{6,5},{7,4},{8,15},{9,14},{10,... | collective-permute-start | bytes 602120 | tf_op jit(solution)/shard_map/ppermute | solution.py:421
  63.8 1.2 %collective-permute-start.6 = (bf16[272,128]{1,0:T(8,128)(2,1)S(1)}, bf16[272,128]{1,0:T(8,128)(2,1)S(1)}, u32[]{:S(2)}, u32[]{:S(2)}) collective-permute-start(bf16[272,128]{1,0:T(8,128)(2,1)S(1)} %get-tuple-element.32), channel_id=1, source_target_pairs={{0,7},{1,6},{2,1},{3,0},{4,3},{5,2},{6,5},{7,4},{8,15},{9,14},{10,... | collective-permute-start | bytes 208904 | tf_op jit(solution)/shard_map/ppermute | solution.py:421
  65.1 11.8 %collective-permute-done.10.refs_2_ = bf16[1040,128]{1,0:T(8,128)(2,1)S(1)} collective-permute-done((bf16[1040,128]{1,0:T(8,128)(2,1)S(1)}, bf16[1040,128]{1,0:T(8,128)(2,1)S(1)}, u32[]{:S(2)}, u32[]{:S(2)}) %collective-permute-start.10) | collective-permute-done | bytes 266272 | tf_op jit(solution)/shard_map/ppermute | solution.py:421
  76.9 2.6 %add_message.11.refs_3_ = f32[8,128,32,128]{3,2,1,0:T(8,128)S(1)} custom-call(s32[9]{0:T(128)S(1)} %stack.39.refs_0_, bf16[8,272,128]{2,1,0:T(8,128)(2,1)S(1)} %all-to-all-done.refs_1_.refs_5_, bf16[1040,128]{1,0:T(8,128)(2,1)S(1)} %collective-permute-done.10.refs_2_, f32[8,128,32,128]{3,2,1,0:T(8,128)S(1)} %get-tuple-element.37.refs_3_), custom_call_target="tpu_custom_call", output_to_operand_aliasing={{}: (3, {})} | custom-call | bytes 1024 | tf_op jit(solution)/shard_map/add_message/pallas_call | solution.py:78
  79.5 0.0 collective-permute-done.9.refs_2_
  79.5 2.6 %add_message.12.refs_3_ = f32[8,128,32,128]{3,2,1,0:T(8,128)S(1)} custom-call(s32[9]{0:T(128)S(1)} %stack.39.refs_0_, bf16[8,272,128]{2,1,0:T(8,128)(2,1)S(1)} %all-to-all-done.refs_1_.refs_5_, bf16[1040,128]{1,0:T(8,128)(2,1)S(1)} %collective-permute-done.9.refs_2_, f32[8,128,32,128]{3,2,1,0:T(8,128)S(1)} %add_message.11.refs_3_), custom_call_target="tpu_custom_call", output_to_operand_aliasing={{}: (3, {})} | custom-call | bytes 1024 | tf_op jit(solution)/shard_map/add_message/pallas_call | solution.py:78
  82.2 0.0 collective-permute-done.8.refs_2_
  82.2 2.6 %add_message.13.refs_3_ = f32[8,128,32,128]{3,2,1,0:T(8,128)S(1)} custom-call(s32[9]{0:T(128)S(1)} %stack.39.refs_0_, bf16[8,272,128]{2,1,0:T(8,128)(2,1)S(1)} %all-to-all-done.refs_1_.refs_5_, bf16[1040,128]{1,0:T(8,128)(2,1)S(1)} %collective-permute-done.8.refs_2_, f32[8,128,32,128]{3,2,1,0:T(8,128)S(1)} %add_message.12.refs_3_), custom_call_target="tpu_custom_call", output_to_operand_aliasing={{}: (3, {})} | custom-call | bytes 1024 | tf_op jit(solution)/shard_map/add_message/pallas_call | solution.py:78
  84.8 0.0 collective-permute-done.7.refs_2_
  84.8 5.2 %add_message.14 = (f32[8,128,32,128]{3,2,1,0:T(8,128)S(1)}, bf16[8,32,16384]{2,1,0:T(8,128)(2,1)}) custom-call(s32[9]{0:T(128)S(1)} %stack.39.refs_0_, bf16[8,272,128]{2,1,0:T(8,128)(2,1)S(1)} %all-to-all-done.refs_1_.refs_5_, bf16[784,128]{1,0:T(8,128)(2,1)S(1)} %collective-permute-done.7.refs_2_, ...), custom_call_target="tpu_custom_call", output_to_operand_aliasing={{0}: (3, {})} | custom-call | bytes 1024 | tf_op jit(solution)/shard_map/add_message/pallas_call | solution.py:78
  90.0 0.0 collective-permute-done.6.refs_2_
  90.0 3.0 %add_message.15 = (f32[8,128,32,128]{3,2,1,0:T(8,128)S(1)}, bf16[8,32,16384]{2,1,0:T(8,128)(2,1)}) custom-call(s32[9]{0:T(128)S(1)} %stack.39.refs_0_, bf16[8,272,128]{2,1,0:T(8,128)(2,1)S(1)} %all-to-all-done.refs_1_.refs_5_, bf16[272,128]{1,0:T(8,128)(2,1)S(1)} %collective-permute-done.6.refs_2_, ...), custom_call_target="tpu_custom_call", output_to_operand_aliasing={{0}: (3, {}), {1}: (4, {})} | custom-call | bytes 1024 | tf_op jit(solution)/shard_map/add_message/pallas_call | solution.py:78
Async XLA Ops:
  0.0 4.4 %collective-permute-start = (s32[4,16]{1,0:T(4,128)}, s32[4,16]{1,0:T(4,128)S(1)}, u32[]{:S(2)}, u32[]{:S(2)}) collective-permute-start(s32[4,16]{1,0:T(4,128)} %bitcast.25), channel_id=1, source_target_pairs={{0,20},{1,21},{2,22},{3,23},{4,16},{5,17},{6,18},{7,19},{8,28},{9,... | collective-permute-start | bytes 776 | tf_op jit(solution)/shard_map/ppermute | solution.py:430
  4.4 0.7 copy-start.1
  6.7 0.9 copy-start
  7.6 0.7 copy-start.2
  10.7 28.4 %all-to-all-start = ((bf16[8,272,128]{2,1,0:T(8,128)(2,1)}), bf16[8,272,128]{2,1,0:T(8,128)(2,1)S(1)}, u32[]{:S(2)}, u32[]{:S(2)}) async-start(bf16[8,272,128]{2,1,0:T(8,128)(2,1)} %get-tuple-element.24), calls=%async_computation | async-start | bytes 1114112 | tf_op jit(solution)/shard_map/all_to_all | solution.py:453
  16.4 22.6 %collective-permute-start.1 = (bf16[1040,128]{1,0:T(8,128)(2,1)S(1)}, bf16[1040,128]{1,0:T(8,128)(2,1)S(1)}, u32[]{:S(2)}, u32[]{:S(2)}) collective-permute-start(bf16[1040,128]{1,0:T(8,128)(2,1)S(1)} %get-tuple-element.25), channel_id=1, source_target_pairs={{0,4},{1,5},{2,6},{3,7},{4,0},{5,1},{6,2},{7,3},{8,12},{9,13},{10,... | collective-permute-start | bytes 798728 | tf_op jit(solution)/shard_map/ppermute | solution.py:421
  16.5 35.2 %collective-permute-start.4 = (bf16[1040,128]{1,0:T(8,128)(2,1)S(1)}, bf16[1040,128]{1,0:T(8,128)(2,1)S(1)}, u32[]{:S(2)}, u32[]{:S(2)}) collective-permute-start(bf16[1040,128]{1,0:T(8,128)(2,1)S(1)} %get-tuple-element.28), channel_id=1, source_target_pairs={{0,5},{1,4},{2,7},{3,6},{4,1},{5,0},{6,3},{7,2},{8,13},{9,12},{10,... | collective-permute-start | bytes 798728 | tf_op jit(solution)/shard_map/ppermute | solution.py:421
  19.3 19.7 %collective-permute-start.2 = (s32[4,16]{1,0:T(4,128)S(1)}, s32[4,16]{1,0:T(4,128)S(1)}, u32[]{:S(2)}, u32[]{:S(2)}) collective-permute-start(s32[4,16]{1,0:T(4,128)S(1)} %get-tuple-element.26.refs_1_.refs_2_), channel_id=1, source_target_pairs={{0,14},{1,15},{2,8},{3,9},{4,10},{5,11},{6,12},{7,13},{8,22},{9,23... | collective-permute-start | bytes 776 | tf_op jit(solution)/shard_map/ppermute | solution.py:430
  42.9 16.3 %collective-permute-start.3 = (bf16[1040,128]{1,0:T(8,128)(2,1)S(1)}, bf16[1040,128]{1,0:T(8,128)(2,1)S(1)}, u32[]{:S(2)}, u32[]{:S(2)}) collective-permute-start(bf16[1040,128]{1,0:T(8,128)(2,1)S(1)} %get-tuple-element.27), channel_id=1, source_target_pairs={{0,2},{1,3},{2,4},{3,5},{4,6},{5,7},{6,0},{7,1},{8,10},{9,11},{10,... | collective-permute-start | bytes 798728 | tf_op jit(solution)/shard_map/ppermute | solution.py:421
  43.0 8.7 %collective-permute-start.5 = (s32[4,16]{1,0:T(4,128)S(1)}, s32[4,16]{1,0:T(4,128)S(1)}, u32[]{:S(2)}, u32[]{:S(2)}) collective-permute-start(s32[4,16]{1,0:T(4,128)S(1)} %get-tuple-element.26.refs_1_.refs_2_), channel_id=1, source_target_pairs={{0,26},{1,27},{2,28},{3,29},{4,30},{5,31},{6,24},{7,25},{8,2},{9,3... | collective-permute-start | bytes 776 | tf_op jit(solution)/shard_map/ppermute | solution.py:430
  54.9 22.0 %collective-permute-start.10 = (bf16[1040,128]{1,0:T(8,128)(2,1)S(1)}, bf16[1040,128]{1,0:T(8,128)(2,1)S(1)}, u32[]{:S(2)}, u32[]{:S(2)}) collective-permute-start(bf16[1040,128]{1,0:T(8,128)(2,1)S(1)} %get-tuple-element.36), channel_id=1, source_target_pairs={{0,3},{1,2},{2,5},{3,4},{4,7},{5,6},{6,1},{7,0},{8,11},{9,10},{10,... | collective-permute-start | bytes 798728 | tf_op jit(solution)/shard_map/ppermute | solution.py:421
  58.1 21.4 %collective-permute-start.9 = (bf16[1040,128]{1,0:T(8,128)(2,1)S(1)}, bf16[1040,128]{1,0:T(8,128)(2,1)S(1)}, u32[]{:S(2)}, u32[]{:S(2)}) collective-permute-start(bf16[1040,128]{1,0:T(8,128)(2,1)S(1)} %get-tuple-element.35), channel_id=1, source_target_pairs={{0,6},{1,7},{2,0},{3,1},{4,2},{5,3},{6,4},{7,5},{8,14},{9,15},{10,... | collective-permute-start | bytes 798728 | tf_op jit(solution)/shard_map/ppermute | solution.py:421
  58.7 23.5 %collective-permute-start.8 = (bf16[1040,128]{1,0:T(8,128)(2,1)S(1)}, bf16[1040,128]{1,0:T(8,128)(2,1)S(1)}, u32[]{:S(2)}, u32[]{:S(2)}) collective-permute-start(bf16[1040,128]{1,0:T(8,128)(2,1)S(1)} %get-tuple-element.34), channel_id=1, source_target_pairs={{0,1},{1,0},{2,3},{3,2},{4,5},{5,4},{6,7},{7,6},{8,9},{9,8},{10,11... | collective-permute-start | bytes 798728 | tf_op jit(solution)/shard_map/ppermute | solution.py:421
  62.4 22.4 %collective-permute-start.7 = (bf16[784,128]{1,0:T(8,128)(2,1)S(1)}, bf16[784,128]{1,0:T(8,128)(2,1)S(1)}, u32[]{:S(2)}, u32[]{:S(2)}) collective-permute-start(bf16[784,128]{1,0:T(8,128)(2,1)S(1)} %get-tuple-element.33), channel_id=1, source_target_pairs={{0,7},{1,6},{2,1},{3,0},{4,3},{5,2},{6,5},{7,4},{8,15},{9,14},{10,... | collective-permute-start | bytes 602120 | tf_op jit(solution)/shard_map/ppermute | solution.py:421
  63.8 26.2 %collective-permute-start.6 = (bf16[272,128]{1,0:T(8,128)(2,1)S(1)}, bf16[272,128]{1,0:T(8,128)(2,1)S(1)}, u32[]{:S(2)}, u32[]{:S(2)}) collective-permute-start(bf16[272,128]{1,0:T(8,128)(2,1)S(1)} %get-tuple-element.32), channel_id=1, source_target_pairs={{0,7},{1,6},{2,1},{3,0},{4,3},{5,2},{6,5},{7,4},{8,15},{9,14},{10,... | collective-permute-start | bytes 208904 | tf_op jit(solution)/shard_map/ppermute | solution.py:421
where the time goes:
time: 93.5 us; the launch traced here: 93 us
  waiting for transfers between devices  38.6 us (41%)
  Pallas kernels  34.1 us (36%)
  starting transfers between devices  17.8 us (19%)
  local copies, waits for them, and re-layouts  2.35 us (3%)
    pallas_call x11, Pallas kernels, kernel_call(): pl.pallas_call(kernel, out_shape=list(outs.values()), in_specs=in_specs,...  34.1 us
    ppermute x3, waiting for transfers between devices, named_by(): return lax.ppermute(cols, ('row', 'col'), pairs)  26.8 us
    ppermute x8, waiting for transfers between devices, step(): return lax.ppermute(value, 'col', pairs)  11.8 us
    ppermute x8, starting transfers between devices, step(): return lax.ppermute(value, 'col', pairs)  9.93 us
    all_to_all x1, starting transfers between devices, on_device(): lax.all_to_all(got['spread'], ('row', 'col'), 0, 0, axis_index_groups=gro...  5.73 us
    unnamed x6, local copies, waits for them, and re-layouts  2.26 us
    ppermute x3, starting transfers between devices, named_by(): return lax.ppermute(cols, ('row', 'col'), pairs)  2.14 us
  transfers between devices with their start and end apart: 12, of which 4 were waited for; matrix products, arithmetic and copies ran while one was open for 0% of the time, Pallas kernels for 29%

commit v1 on v0

--- a/solution.py
+++ b/solution.py
@@ -89,7 +89,7 @@
     return dict(zip(outs, got))
 
 
-FLOPS = 0
+FLOPS = 2 * 10**10
 
 
 class Gather:
@@ -186,9 +186,9 @@
             move.wait()
         lane_block = lax.broadcasted_iota(I32, (z.bs, LANES), 1) // z.bs
 
-        def one_row(i, _):
+        for i in range(first, last):
             for m in range(z.ra):
-                value = prod[pl.ds(pl.multiple_of(((i - first) * z.ra + m) * z.bs, z.bs), z.bs), :]
+                value = prod[pl.ds(((i - first) * z.ra + m) * z.bs, z.bs), :]
                 placed = []
                 for n in range(z.rb):
                     entry = (n * z.ra + m) * z.half + i
@@ -199,9 +199,6 @@
                     placed.append((column // per, moved))
                 for tile, moved in placed:
                     acc[i, tile] = acc[i, tile] + moved
-            return 0
-
-        lax.fori_loop(first, last, one_row, 0)
 
 
 def clear(acc):
@@ -235,69 +232,99 @@
         send(at).wait()
 
 
-def first_answer(z, info, cols, own_cols, b_scl, b_pos, b, rows):
+def first_answers(z, info, cols, b_scl, b_pos, b, rows, after):
     rb, kw = b_scl.shape
 
     def body(refs):
-        answer = Gather(z, refs, "message", 0, rows, "cols", refs["sems"].at[0])
+        answers = [
+            Gather(z, refs, f"message{flip}", flip, rows, "cols", refs["sems"].at[flip]) for flip in range(2)
+        ]
         moves = [
-            pltpu.make_async_copy(refs["b_scl"], refs["scl"], refs["sems"].at[1]),
-            pltpu.make_async_copy(refs["b_pos"], refs["pos"], refs["sems"].at[2]),
+            pltpu.make_async_copy(refs["b_scl"], refs["scl"], refs["sems"].at[2]),
+            pltpu.make_async_copy(refs["b_pos"], refs["pos"], refs["sems"].at[3]),
         ]
         for move in moves:
             move.start()
-        answer.start()
-        refs["own"][...] = refs["own_cols"][...]
+        for answer in answers:
+            answer.start()
         for move in moves:
             move.wait()
         scale, column = refs["scl"][...], refs["pos"][...]
         table = three_parts(scale) + [(column >> 8).astype(F32), (column & 255).astype(F32)]
         table.append(jnp.zeros((refs["table"].shape[0] - PARTS * rb, kw), F32))
         refs["table"][...] = jnp.concatenate(table, axis=0).astype(BF16)
-        answer.finish()
-
+        for answer in answers:
+            answer.finish()
+
+    ins = {
+        "info": (info, "smem"),
+        "cols_s": (cols, "smem"),
+        "cols_v": (cols, "vmem"),
+        "b_scl": (b_scl, "hbm"),
+        "b_pos": (b_pos, "hbm"),
+        "b": (b, "hbm"),
+    }
+    ins.update({f"after{at}": (array, "any") for at, array in enumerate(after)})
     return kernel_call(
-        "first_answer",
+        "first_answers",
         body,
-        {
-            "info": (info, "smem"),
-            "cols_s": (cols, "smem"),
-            "cols_v": (cols, "vmem"),
-            "own_cols": (own_cols, "vmem"),
-            "b_scl": (b_scl, "hbm"),
-            "b_pos": (b_pos, "hbm"),
-            "b": (b, "hbm"),
-        },
+        ins,
         {
             "table": pltpu.VMEM((-(-PARTS * rb // 16) * 16, kw), BF16),
-            "message": z.message(rows),
-            "own": pltpu.VMEM(own_cols.shape, I32),
+            "message0": z.message(rows),
+            "message1": z.message(rows),
         },
         scratch={
             "scl": pltpu.VMEM(b_scl.shape, F32),
             "pos": pltpu.VMEM(b_pos.shape, I32),
-            "sems": pltpu.SemaphoreType.DMA((3,)),
+            "sems": pltpu.SemaphoreType.DMA((4,)),
         },
     )
 
 
-def second_answer(z, info, cols, table, b, rows, a, a_scl, panels):
+def split(z, info, a, a_scl, after):
     def body(refs):
-        answer = Gather(z, refs, "message", 1, rows, "cols", refs["sems"].at[0])
-        answer.start()
         scale = refs["a_scl"][...]
+        both = [entries(scale, h * z.half, z.half, z.rb) for h in range(2)]
         size = z.half * z.bs
-        spread = refs["spread"]
-        for side in range(2):
-            blocks = refs["a"][pl.ds(side * size, size), :]
-            scales = stacked(three_parts(entries(scale, side * z.half, z.half, z.rb)), META).astype(BF16)
-            for panel in range(panels):
-                spread[2 * panel + side, pl.ds(0, size), :] = blocks
-                spread[2 * panel + side, pl.ds(size, META), :] = scales
-        answer.finish()
-
+        for flip, out in enumerate((refs["kept"], refs["given"])):
+            side = refs["info"][0] ^ flip
+            out[0, pl.ds(0, size), :] = refs["a"][pl.ds(pl.multiple_of(side * size, size), size), :]
+            parts = three_parts(jnp.where(side == 1, both[1], both[0]))
+            out[0, pl.ds(size, META), :] = stacked(parts, META).astype(BF16)
+
+    piece = pltpu.VMEM((1, z.half * z.bs + META, z.wide), BF16)
     return kernel_call(
-        "second_answer",
+        "split",
+        body,
+        {"info": (info, "smem"), "a": (a, "vmem"), "a_scl": (a_scl, "vmem"), "after": (after, "any")},
+        {"kept": piece, "given": piece},
+    )
+
+
+def join(own, taken):
+    count = own.shape[0]
+
+    def body(refs):
+        refs["both"][pl.ds(0, count)] = refs["own"][...]
+        refs["both"][pl.ds(count, count)] = refs["taken"][...]
+
+    outs = {"both": pltpu.VMEM((2 * count,) + own.shape[1:], BF16)}
+    return kernel_call("join", body, {"own": (own, "vmem"), "taken": (taken, "vmem")}, outs)["both"]
+
+
+def more_answers(z, info, cols, table, b, rows, after):
+    def body(refs):
+        answers = [
+            Gather(z, refs, f"message{flip}", flip, rows, "cols", refs["sems"].at[flip]) for flip in range(2)
+        ]
+        for answer in answers:
+            answer.start()
+        for answer in answers:
+            answer.finish()
+
+    return kernel_call(
+        "more_answers",
         body,
         {
             "info": (info, "smem"),
@@ -305,25 +332,22 @@
             "cols_v": (cols, "vmem"),
             "table": (table, "vmem"),
             "b": (b, "hbm"),
-            "a": (a, "vmem"),
-            "a_scl": (a_scl, "vmem"),
+            "after": (after, "any"),
         },
-        {
-            "message": z.message(rows),
-            "spread": pltpu.VMEM((2 * panels, z.half * z.bs + META, z.wide), BF16),
-        },
-        scratch={"sems": pltpu.SemaphoreType.DMA((1,))},
-    )
-
-
-def own_blocks(z, info, cols, table, b, rows, left, acc):
+        {"message0": z.message(rows), "message1": z.message(rows)},
+        scratch={"sems": pltpu.SemaphoreType.DMA((2,))},
+    )
+
+
+def own_blocks(z, info, cols, table, b, rows, kept, after):
     def body(refs):
         answer = Gather(z, refs, "message", 1, rows, "cols", refs["sems"].at[0])
         local = Gather(z, refs, "local", 0, rows, "cols", refs["sems"].at[1])
         local.start()
         answer.start()
+        clear(refs["acc"])
         local.finish()
-        add = Add(z, refs, refs["left"].at[refs["info"][1]], refs["local"], rows)
+        add = Add(z, refs, refs["kept"].at[0], refs["local"], rows)
         add.start()
         answer.finish()
         add.finish()
@@ -337,11 +361,10 @@
             "cols_v": (cols, "vmem"),
             "table": (table, "vmem"),
             "b": (b, "hbm"),
-            "left": (left, "vmem"),
-            "acc_in": (acc, "vmem"),
+            "kept": (kept, "vmem"),
+            "after": (after, "any"),
         },
         {"acc": z.window(), "message": z.message(rows)},
-        aliases=[("acc_in", "acc")],
         scratch={
             "sems": pltpu.SemaphoreType.DMA((2,)),
             "local": z.message(rows),
@@ -350,17 +373,15 @@
     )
 
 
-def add_message(z, info, left, by, flip, message, rows, acc, answers=(), table=None, b=None, write=False, out=None):
+def add_message(z, info, left, by, flip, message, rows, acc, answers=(), table=None, b=None, write=False, out=None, after=()):
     ins = {
         "info": (info, "smem"),
         "left": (left, "vmem"),
         "arrived": (message, "vmem"),
+        "acc_in": (acc, "vmem"),
     }
     outs = {"acc": z.window()}
-    aliases = []
-    if acc is not None:
-        ins["acc_in"] = (acc, "vmem")
-        aliases.append(("acc_in", "acc"))
+    aliases = [("acc_in", "acc")]
     scratch = Add.scratch(z, rows)
     if answers:
         ins.update(table=(table, "vmem"), b=(b, "hbm"))
@@ -369,6 +390,7 @@
         ins[f"cols{at}_s"] = (cols, "smem")
         ins[f"cols{at}_v"] = (cols, "vmem")
         outs[f"message{at}"] = z.message(span)
+    ins.update({f"after{at}": (array, "any") for at, array in enumerate(after)})
     if write:
         outs["out"] = jax.ShapeDtypeStruct((z.half, z.bs, JW * z.bs), BF16)
         scratch["stage"] = pltpu.VMEM((8, z.bs, JW * z.bs // CHUNKS), BF16)
@@ -384,11 +406,9 @@
         ]
         for gather in gathers:
             gather.start()
-        place = refs["info"][1 + 2 * by + flip]
+        place = flip if by == 0 else refs["info"][1 + by] * 2 + flip
         add = Add(z, refs, refs["left"].at[place], refs["arrived"], rows)
         add.start()
-        if acc is None:
-            clear(refs["acc"])
         for gather in gathers:
             gather.finish()
         add.finish()
@@ -411,8 +431,7 @@
     z = Sizes(half, a_scl.shape[0], b_scl.shape[0], bs)
     row = lax.axis_index("row")
     parity = lax.axis_index("col") % halves
-    places = [(row - by) % panels * halves + (parity ^ flip) for by in range(panels) for flip in range(halves)]
-    info = jnp.stack([parity] + places).astype(I32)
+    info = jnp.stack([parity] + [row ^ ((row - by) % panels) for by in range(panels)]).astype(I32)
 
     def step(value, by, flip):
         pairs = [
@@ -420,60 +439,60 @@
         ]
         return lax.ppermute(value, "col", pairs)
 
-    def named_by(by, cols):
+    def named_by(by):
         pairs = []
         for r in range(panels):
             for c in range(columns):
                 to_row = (r + by) % panels
                 to_col = (c - halves * by) % columns
                 pairs.append((r * columns + c, to_row * columns + to_col))
-        return lax.ppermute(cols, ("row", "col"), pairs)
+        return lax.ppermute(a_pos, ("row", "col"), pairs)
 
     order = sorted(range(1, panels), key=lambda by: -min(by, panels - by))
     every = (0, half)
     early = (0, half - max(1, half // 4))
     late = (early[1], half)
-    queue = [(by, flip, every) for by in order for flip in range(halves)]
-    queue[-1:] = [(order[-1], 1, early), (order[-1], 1, late)]
-
-    asked = {order[0]: named_by(order[0], a_pos)}
-    got = first_answer(z, info, asked[order[0]], a_pos, b_scl, b_pos, b_part, every)
-    table, own_cols = got["table"], got["own"]
-    moving = [step(got["message"], order[0], 0)]
-    for by in order[1:]:
-        asked[by] = named_by(by, own_cols)
-    a_flat = a_part.reshape(nrows * bs, z.wide)
-    got = second_answer(z, info, asked[order[0]], table, b_part, every, a_flat, a_scl, panels)
-    moving.append(step(got["message"], order[0], 1))
-
-    groups = [
-        [r * columns + c for r in range(panels) for c in range(s * halves, (s + 1) * halves)]
-        for s in range(panels)
-    ]
-    left = lax.all_to_all(got["spread"], ("row", "col"), 0, 0, axis_index_groups=groups)
-
-    acc = None
-    taken = None
-    out = None
-    for at, (by, flip, rows) in enumerate(queue):
-        upto = min(len(queue), at + (3 if at == 0 else 4))
-        if upto == len(queue) - 1:
-            upto = len(queue)
-        later = queue[len(moving) : upto]
-        if at == len(queue) - 2:
-            acc = add_message(z, info, left, 0, 1, taken, every, acc)[0]
-        write = at >= len(queue) - 2
-        acc, answers, out = add_message(
-            z, info, left, by, flip, moving[at], rows, acc,
-            answers=[(asked[to], side, span) for to, side, span in later],
-            table=table, b=b_part, write=write, out=out,
-        )
-        for answer, (to, side, _) in zip(answers, later):
-            moving.append(step(answer, to, side))
-        if at == 0:
-            mine = own_blocks(z, info, own_cols, table, b_part, every, left, acc)
-            acc = mine["acc"]
-            taken = step(mine["message"], 0, 1)
+    last = order[-1]
+    asked = {by: named_by(by) for by in order}
+
+    got = first_answers(
+        z, info, asked[order[0]], b_scl, b_pos, b_part, every, [asked[by] for by in order[1:]]
+    )
+    table = got["table"]
+    moving = {(order[0], flip): step(got[f"message{flip}"], order[0], flip) for flip in range(halves)}
+    pieces = split(z, info, a_part.reshape(nrows * bs, z.wide), a_scl, got["message0"])
+    own_left = join(pieces["kept"], step(pieces["given"], 0, 1))
+    left = own_left
+    bit = 1
+    while bit < panels:
+        left = join(left, lax.ppermute(left, "row", [(r, r ^ bit) for r in range(panels)]))
+        bit *= 2
+    after = got["message0"]
+    for by in order[1:-1]:
+        got = more_answers(z, info, asked[by], table, b_part, every, after)
+        after = got["message0"]
+        for flip in range(halves):
+            moving[by, flip] = step(got[f"message{flip}"], by, flip)
+
+    mine = own_blocks(z, info, a_pos, table, b_part, every, pieces["kept"], after)
+    taken = step(mine["message"], 0, 1)
+    more = {"table": table, "b": b_part}
+    acc, answers, _ = add_message(
+        z, info, own_left, 0, 1, taken, every, mine["acc"], [(asked[last], 0, every)], **more
+    )
+    ends = answers
+    for by in order[:-1]:
+        for flip in range(halves):
+            first = by == order[0]
+            acc, answers, _ = add_message(
+                z, info, left, by, flip, moving[by, flip], every, acc,
+                [(asked[last], 1, late if flip else early)] if first else [],
+                after=ends[-1:] if first else [], **(more if first else {}),
+            )
+            ends += answers
+    acc = add_message(z, info, left, last, 0, step(ends[0], last, 0), every, acc)[0]
+    acc, _, out = add_message(z, info, left, last, 1, step(ends[1], last, 1), early, acc, write=True)
+    out = add_message(z, info, left, last, 1, step(ends[2], last, 1), late, acc, write=True, out=out)[2]
     return out[None, None]
 
 

time: 93.5 us -> 73.9 us (0.79)
  the two profiles are of different devices: /device:TPU:19 before, /device:TPU:0 now
where the time goes in v1:
time: 73.9 us; the launch traced here: 73.5 us
  Pallas kernels  30.6 us (41%)
  starting transfers between devices  26 us (35%)
  waiting for transfers between devices  16.4 us (22%)
    pallas_call x15, Pallas kernels, kernel_call(): pl.pallas_call(kernel, out_shape=list(outs.values()), in_specs=in_specs,...  30.6 us
    ppermute x9, starting transfers between devices, step(): return lax.ppermute(value, 'col', pairs)  15.1 us
    ppermute x9, waiting for transfers between devices, step(): return lax.ppermute(value, 'col', pairs)  8.23 us
    ppermute x3, starting transfers between devices, named_by(): return lax.ppermute(a_pos, ('row', 'col'), pairs)  7.92 us
    ppermute x2, waiting for transfers between devices, on_device(): lax.ppermute(left, 'row', [(r, r ^ bit) for r in range(panels)])  4.64 us
    ppermute x3, waiting for transfers between devices, named_by(): return lax.ppermute(a_pos, ('row', 'col'), pairs)  3.57 us
    ppermute x2, starting transfers between devices, on_device(): lax.ppermute(left, 'row', [(r, r ^ bit) for r in range(panels)])  2.99 us
  transfers between devices with their start and end apart: 14, of which 6 were waited for; matrix products, arithmetic and copies ran while one was open for 0% of the time, Pallas kernels for 35%

profile of v1, /device:TPU:0, one launch (start us, length us, event | category | flops | bytes accessed | tf_op | source)
XLA Modules:
  0.0 73.5 jit_solution(12847538055925065150)
XLA Ops:
  0.0 4.9 %collective-permute-start.2 = (s32[4,16]{1,0:T(4,128)}, s32[4,16]{1,0:T(4,128)S(1)}, u32[]{:S(2)}, u32[]{:S(2)}) collective-permute-start(s32[4,16]{1,0:T(4,128)} %bitcast.22), channel_id=1, source_target_pairs={{0,26},{1,27},{2,28},{3,29},{4,30},{5,31},{6,24},{7,25},{8,2},{9,3... | collective-permute-start | bytes 776 | tf_op jit(solution)/shard_map/ppermute | solution.py:449
  4.9 1.1 %collective-permute-start.1 = (s32[4,16]{1,0:T(4,128)}, s32[4,16]{1,0:T(4,128)S(1)}, u32[]{:S(2)}, u32[]{:S(2)}) collective-permute-start(s32[4,16]{1,0:T(4,128)} %bitcast.23), channel_id=1, source_target_pairs={{0,14},{1,15},{2,8},{3,9},{4,10},{5,11},{6,12},{7,13},{8,22},{9,23... | collective-permute-start | bytes 776 | tf_op jit(solution)/shard_map/ppermute | solution.py:449
  6.0 1.9 %collective-permute-start = (s32[4,16]{1,0:T(4,128)}, s32[4,16]{1,0:T(4,128)S(1)}, u32[]{:S(2)}, u32[]{:S(2)}) collective-permute-start(s32[4,16]{1,0:T(4,128)} %bitcast.24), channel_id=1, source_target_pairs={{0,20},{1,21},{2,22},{3,23},{4,16},{5,17},{6,18},{7,19},{8,28},{9,... | collective-permute-start | bytes 776 | tf_op jit(solution)/shard_map/ppermute | solution.py:449
  7.9 0.1 stack.23.refs_0_
  8.0 0.0 collective-permute-done.2.refs_7_.refs_6_
  8.0 2.5 %collective-permute-done.1.refs_6_.refs_1_.refs_2_ = s32[4,16]{1,0:T(4,128)S(1)} collective-permute-done((s32[4,16]{1,0:T(4,128)}, s32[4,16]{1,0:T(4,128)S(1)}, u32[]{:S(2)}, u32[]{:S(2)}) %collective-permute-start.1) | collective-permute-done | bytes 288 | tf_op jit(solution)/shard_map/ppermute | solution.py:449
  10.5 1.1 %collective-permute-done.refs_1_.refs_2_ = s32[4,16]{1,0:T(4,128)S(1)} collective-permute-done((s32[4,16]{1,0:T(4,128)}, s32[4,16]{1,0:T(4,128)S(1)}, u32[]{:S(2)}, u32[]{:S(2)}) %collective-permute-start) | collective-permute-done | bytes 288 | tf_op jit(solution)/shard_map/ppermute | solution.py:449
  11.6 0.0 copy-start
  11.6 0.0 copy-start.1
  11.6 1.9 %first_answers.1 = (bf16[32,1024]{1,0:T(8,128)(2,1)S(1)}, bf16[1040,128]{1,0:T(8,128)(2,1)S(1)}, bf16[1040,128]{1,0:T(8,128)(2,1)S(1)}) custom-call(s32[5]{0:T(128)S(1)} %stack.23.refs_0_, s32[4,16]{1,0:T(4,128)S(1)} %collective-permute-done.refs_1_.refs_2_, s32[4,16]{1,0:T(4,128)S(1)} %collective-permute-done.refs_1_.refs_2_, f32[4,1024]{1,0:T(4,128)} %bitcast.33, ...), custom_call_target="tpu_custom_call" | custom-call | flops 20000000000 | bytes 1024 | tf_op jit(solution)/shard_map/first_answers/pallas_call | solution.py:78
  13.5 1.6 %collective-permute-start.7 = (bf16[1040,128]{1,0:T(8,128)(2,1)S(1)}, bf16[1040,128]{1,0:T(8,128)(2,1)S(1)}, u32[]{:S(2)}, u32[]{:S(2)}) collective-permute-start(bf16[1040,128]{1,0:T(8,128)(2,1)S(1)} %get-tuple-element.23.refs_3_.refs_5_), channel_id=1, source_target_pairs={{0,4},{1,5},{2,6},{3,7},{4,0},{5,1},{6,2},{7,3},{8,12},{9,13},{10,... | collective-permute-start | bytes 798728 | tf_op jit(solution)/shard_map/ppermute | solution.py:440
  15.1 0.0 copy-done
  15.1 0.0 copy-done.1
  15.1 0.6 split.1
  15.7 0.1 collective-permute-start.3
  15.8 1.8 %more_answers.1 = (bf16[1040,128]{1,0:T(8,128)(2,1)S(1)}, bf16[1040,128]{1,0:T(8,128)(2,1)S(1)}) custom-call(s32[5]{0:T(128)S(1)} %stack.23.refs_0_, s32[4,16]{1,0:T(4,128)S(1)} %collective-permute-done.1.refs_6_.refs_1_.refs_2_, s32[4,16]{1,0:T(4,128)S(1)} %collective-permute-done.1.refs_6_.refs_1_.refs_2_, ...), custom_call_target="tpu_custom_call" | custom-call | flops 20000000000 | bytes 1024 | tf_op jit(solution)/shard_map/more_answers/pallas_call | solution.py:78
  17.6 2.1 %collective-permute-start.13 = (bf16[1040,128]{1,0:T(8,128)(2,1)S(1)}, bf16[1040,128]{1,0:T(8,128)(2,1)S(1)}, u32[]{:S(2)}, u32[]{:S(2)}) collective-permute-start(bf16[1040,128]{1,0:T(8,128)(2,1)S(1)} %get-tuple-element.28.refs_6_), channel_id=1, source_target_pairs={{0,2},{1,3},{2,4},{3,5},{4,6},{5,7},{6,0},{7,1},{8,10},{9,11},{10,... | collective-permute-start | bytes 798728 | tf_op jit(solution)/shard_map/ppermute | solution.py:440
  19.7 0.0 collective-permute-done.3.refs_1_
  19.7 0.0 copy-start.2
  19.7 1.5 %collective-permute-start.4 = (bf16[2,272,128]{2,1,0:T(8,128)(2,1)S(1)}, bf16[2,272,128]{2,1,0:T(8,128)(2,1)S(1)}, u32[]{:S(2)}, u32[]{:S(2)}) collective-permute-start(bf16[2,272,128]{2,1,0:T(8,128)(2,1)S(1)} %join.3.refs_0_.refs_1_), channel_id=1, source_target_pairs={{0,8},{8,0},{16,24},{24,16},{1,9},{9,1},{17,25},{25,17},{2,10},{10... | collective-permute-start | bytes 417800 | tf_op jit(solution)/shard_map/ppermute | solution.py:468
  21.2 0.0 copy-done.2
  21.2 4.2 %own_blocks.1 = (f32[8,128,32,128]{3,2,1,0:T(8,128)S(1)}, bf16[1040,128]{1,0:T(8,128)(2,1)S(1)}) custom-call(s32[5]{0:T(128)S(1)} %stack.23.refs_0_, s32[4,16]{1,0:T(4,128)S(1)} %bitcast.25, s32[4,16]{1,0:T(4,128)S(1)} %bitcast.26, bf16[32,1024]{1,0:T(8,128)(2,1)S(1)} %get-tuple-element.27.refs_3_.refs_4_, bf16[1024,32,128]{2,1,0:T(8,128)(2,1)} %bitcast.29, ...), custom_call_target="tpu_custom_call" | custom-call | flops 20000000000 | bytes 1024 | tf_op jit(solution)/shard_map/own_blocks/pallas_call | solution.py:78
  25.4 0.5 collective-permute-start.6
  25.9 2.1 %collective-permute-start.12 = (bf16[1040,128]{1,0:T(8,128)(2,1)S(1)}, bf16[1040,128]{1,0:T(8,128)(2,1)S(1)}, u32[]{:S(2)}, u32[]{:S(2)}) collective-permute-start(bf16[1040,128]{1,0:T(8,128)(2,1)S(1)} %get-tuple-element.36), channel_id=1, source_target_pairs={{0,3},{1,2},{2,5},{3,4},{4,7},{5,6},{6,1},{7,0},{8,11},{9,10},{10,... | collective-permute-start | bytes 798728 | tf_op jit(solution)/shard_map/ppermute | solution.py:440
  28.0 0.0 collective-permute-done.4.refs_1_
  28.0 0.0 collective-permute-start.8
  28.1 1.5 %collective-permute-done.8.refs_2_ = bf16[1040,128]{1,0:T(8,128)(2,1)S(1)} collective-permute-done((bf16[1040,128]{1,0:T(8,128)(2,1)S(1)}, bf16[1040,128]{1,0:T(8,128)(2,1)S(1)}, u32[]{:S(2)}, u32[]{:S(2)}) %collective-permute-start.8) | collective-permute-done | bytes 266272 | tf_op jit(solution)/shard_map/ppermute | solution.py:440
  29.6 1.5 %collective-permute-start.5 = (bf16[4,272,128]{2,1,0:T(8,128)(2,1)S(1)}, bf16[4,272,128]{2,1,0:T(8,128)(2,1)S(1)}, u32[]{:S(2)}, u32[]{:S(2)}) collective-permute-start(bf16[4,272,128]{2,1,0:T(8,128)(2,1)S(1)} %join.4.refs_0_), channel_id=1, source_target_pairs={{0,16},{8,24},{16,0},{24,8},{1,17},{9,25},{17,1},{25,9},{2,18},{10... | collective-permute-start | bytes 835592 | tf_op jit(solution)/shard_map/ppermute | solution.py:468
  31.1 2.5 %add_message.8 = (f32[8,128,32,128]{3,2,1,0:T(8,128)S(1)}, bf16[1040,128]{1,0:T(8,128)(2,1)S(1)}) custom-call(s32[5]{0:T(128)S(1)} %stack.23.refs_0_, bf16[2,272,128]{2,1,0:T(8,128)(2,1)S(1)} %join.3.refs_0_.refs_1_, bf16[1040,128]{1,0:T(8,128)(2,1)S(1)} %collective-permute-done.8.refs_2_, ...), custom_call_target="tpu_custom_call", output_to_operand_aliasing={{0}: (3, {})} | custom-call | flops 20000000000 | bytes 1024 | tf_op jit(solution)/shard_map/add_message/pallas_call | solution.py:78
  33.6 4.6 %collective-permute-done.5.refs_1_ = bf16[4,272,128]{2,1,0:T(8,128)(2,1)S(1)} collective-permute-done((bf16[4,272,128]{2,1,0:T(8,128)(2,1)S(1)}, bf16[4,272,128]{2,1,0:T(8,128)(2,1)S(1)}, u32[]{:S(2)}, u32[]{:S(2)}) %collective-permute-start.5) | collective-permute-done | bytes 278560 | tf_op jit(solution)/shard_map/ppermute | solution.py:468
  38.3 1.7 %collective-permute-start.11 = (bf16[1040,128]{1,0:T(8,128)(2,1)S(1)}, bf16[1040,128]{1,0:T(8,128)(2,1)S(1)}, u32[]{:S(2)}, u32[]{:S(2)}) collective-permute-start(bf16[1040,128]{1,0:T(8,128)(2,1)S(1)} %get-tuple-element.32.refs_8_), channel_id=1, source_target_pairs={{0,6},{1,7},{2,0},{3,1},{4,2},{5,3},{6,4},{7,5},{8,14},{9,15},{10,... | collective-permute-start | bytes 798728 | tf_op jit(solution)/shard_map/ppermute | solution.py:440
  40.0 4.6 %collective-permute-done.7.refs_2_ = bf16[1040,128]{1,0:T(8,128)(2,1)S(1)} collective-permute-done((bf16[1040,128]{1,0:T(8,128)(2,1)S(1)}, bf16[1040,128]{1,0:T(8,128)(2,1)S(1)}, u32[]{:S(2)}, u32[]{:S(2)}) %collective-permute-start.7) | collective-permute-done | bytes 266272 | tf_op jit(solution)/shard_map/ppermute | solution.py:440
  44.6 2.5 %add_message.9 = (f32[8,128,32,128]{3,2,1,0:T(8,128)S(1)}, bf16[784,128]{1,0:T(8,128)(2,1)S(1)}) custom-call(s32[5]{0:T(128)S(1)} %stack.23.refs_0_, bf16[8,272,128]{2,1,0:T(8,128)(2,1)S(1)} %join.5.refs_1_, bf16[1040,128]{1,0:T(8,128)(2,1)S(1)} %collective-permute-done.7.refs_2_, ...), custom_call_target="tpu_custom_call", output_to_operand_aliasing={{0}: (3, {})} | custom-call | flops 20000000000 | bytes 1024 | tf_op jit(solution)/shard_map/add_message/pallas_call | solution.py:78
  47.1 0.1 collective-permute-start.10
  47.1 2.1 %collective-permute-done.6.refs_2_ = bf16[1040,128]{1,0:T(8,128)(2,1)S(1)} collective-permute-done((bf16[1040,128]{1,0:T(8,128)(2,1)S(1)}, bf16[1040,128]{1,0:T(8,128)(2,1)S(1)}, u32[]{:S(2)}, u32[]{:S(2)}) %collective-permute-start.6) | collective-permute-done | bytes 266272 | tf_op jit(solution)/shard_map/ppermute | solution.py:440
  49.3 2.6 %add_message.10 = (f32[8,128,32,128]{3,2,1,0:T(8,128)S(1)}, bf16[272,128]{1,0:T(8,128)(2,1)S(1)}) custom-call(s32[5]{0:T(128)S(1)} %stack.23.refs_0_, bf16[8,272,128]{2,1,0:T(8,128)(2,1)S(1)} %join.5.refs_1_, bf16[1040,128]{1,0:T(8,128)(2,1)S(1)} %collective-permute-done.6.refs_2_, ...), custom_call_target="tpu_custom_call", output_to_operand_aliasing={{0}: (3, {})} | custom-call | flops 20000000000 | bytes 1024 | tf_op jit(solution)/shard_map/add_message/pallas_call | solution.py:78
  51.8 7.0 %collective-permute-start.9 = (bf16[272,128]{1,0:T(8,128)(2,1)S(1)}, bf16[272,128]{1,0:T(8,128)(2,1)S(1)}, u32[]{:S(2)}, u32[]{:S(2)}) collective-permute-start(bf16[272,128]{1,0:T(8,128)(2,1)S(1)} %get-tuple-element.35), channel_id=1, source_target_pairs={{0,7},{1,6},{2,1},{3,0},{4,3},{5,2},{6,5},{7,4},{8,15},{9,14},{10,... | collective-permute-start | bytes 208904 | tf_op jit(solution)/shard_map/ppermute | solution.py:440
  58.9 0.0 collective-permute-done.13.refs_2_
  58.9 2.2 %add_message.11.refs_3_ = f32[8,128,32,128]{3,2,1,0:T(8,128)S(1)} custom-call(s32[5]{0:T(128)S(1)} %stack.23.refs_0_, bf16[8,272,128]{2,1,0:T(8,128)(2,1)S(1)} %join.5.refs_1_, bf16[1040,128]{1,0:T(8,128)(2,1)S(1)} %collective-permute-done.13.refs_2_, f32[8,128,32,128]{3,2,1,0:T(8,128)S(1)} %get-tuple-element.37.refs_3_), custom_call_target="tpu_custom_call", output_to_operand_aliasing={{}: (3, {})} | custom-call | flops 20000000000 | bytes 1024 | tf_op jit(solution)/shard_map/add_message/pallas_call | solution.py:78
  61.1 0.0 collective-permute-done.12.refs_2_
  61.1 2.2 %add_message.12.refs_3_ = f32[8,128,32,128]{3,2,1,0:T(8,128)S(1)} custom-call(s32[5]{0:T(128)S(1)} %stack.23.refs_0_, bf16[8,272,128]{2,1,0:T(8,128)(2,1)S(1)} %join.5.refs_1_, bf16[1040,128]{1,0:T(8,128)(2,1)S(1)} %collective-permute-done.12.refs_2_, f32[8,128,32,128]{3,2,1,0:T(8,128)S(1)} %add_message.11.refs_3_), custom_call_target="tpu_custom_call", output_to_operand_aliasing={{}: (3, {})} | custom-call | flops 20000000000 | bytes 1024 | tf_op jit(solution)/shard_map/add_message/pallas_call | solution.py:78
  63.3 0.0 collective-permute-done.11.refs_2_
  63.4 2.2 %add_message.13.refs_3_ = f32[8,128,32,128]{3,2,1,0:T(8,128)S(1)} custom-call(s32[5]{0:T(128)S(1)} %stack.23.refs_0_, bf16[8,272,128]{2,1,0:T(8,128)(2,1)S(1)} %join.5.refs_1_, bf16[1040,128]{1,0:T(8,128)(2,1)S(1)} %collective-permute-done.11.refs_2_, f32[8,128,32,128]{3,2,1,0:T(8,128)S(1)} %add_message.12.refs_3_), custom_call_target="tpu_custom_call", output_to_operand_aliasing={{}: (3, {})} | custom-call | flops 20000000000 | bytes 1024 | tf_op jit(solution)/shard_map/add_message/pallas_call | solution.py:78
  65.6 0.0 collective-permute-done.10.refs_2_
  65.6 4.8 %add_message.14 = (f32[8,128,32,128]{3,2,1,0:T(8,128)S(1)}, bf16[8,32,16384]{2,1,0:T(8,128)(2,1)}) custom-call(s32[5]{0:T(128)S(1)} %stack.23.refs_0_, bf16[8,272,128]{2,1,0:T(8,128)(2,1)S(1)} %join.5.refs_1_, bf16[784,128]{1,0:T(8,128)(2,1)S(1)} %collective-permute-done.10.refs_2_, ...), custom_call_target="tpu_custom_call", output_to_operand_aliasing={{0}: (3, {})} | custom-call | flops 20000000000 | bytes 1024 | tf_op jit(solution)/shard_map/add_message/pallas_call | solution.py:78
  70.4 0.0 collective-permute-done.9.refs_2_
  70.5 2.9 %add_message.15 = (f32[8,128,32,128]{3,2,1,0:T(8,128)S(1)}, bf16[8,32,16384]{2,1,0:T(8,128)(2,1)}) custom-call(s32[5]{0:T(128)S(1)} %stack.23.refs_0_, bf16[8,272,128]{2,1,0:T(8,128)(2,1)S(1)} %join.5.refs_1_, bf16[272,128]{1,0:T(8,128)(2,1)S(1)} %collective-permute-done.9.refs_2_, ...), custom_call_target="tpu_custom_call", output_to_operand_aliasing={{0}: (3, {}), {1}: (4, {})} | custom-call | flops 20000000000 | bytes 1024 | tf_op jit(solution)/shard_map/add_message/pallas_call | solution.py:78
  (3 shorter events, 0.1 us)
Async XLA Ops:
  0.0 8.0 %collective-permute-start.2 = (s32[4,16]{1,0:T(4,128)}, s32[4,16]{1,0:T(4,128)S(1)}, u32[]{:S(2)}, u32[]{:S(2)}) collective-permute-start(s32[4,16]{1,0:T(4,128)} %bitcast.22), channel_id=1, source_target_pairs={{0,26},{1,27},{2,28},{3,29},{4,30},{5,31},{6,24},{7,25},{8,2},{9,3... | collective-permute-start | bytes 776 | tf_op jit(solution)/shard_map/ppermute | solution.py:449
  4.9 5.6 %collective-permute-start.1 = (s32[4,16]{1,0:T(4,128)}, s32[4,16]{1,0:T(4,128)S(1)}, u32[]{:S(2)}, u32[]{:S(2)}) collective-permute-start(s32[4,16]{1,0:T(4,128)} %bitcast.23), channel_id=1, source_target_pairs={{0,14},{1,15},{2,8},{3,9},{4,10},{5,11},{6,12},{7,13},{8,22},{9,23... | collective-permute-start | bytes 776 | tf_op jit(solution)/shard_map/ppermute | solution.py:449
  6.0 5.6 %collective-permute-start = (s32[4,16]{1,0:T(4,128)}, s32[4,16]{1,0:T(4,128)S(1)}, u32[]{:S(2)}, u32[]{:S(2)}) collective-permute-start(s32[4,16]{1,0:T(4,128)} %bitcast.24), channel_id=1, source_target_pairs={{0,20},{1,21},{2,22},{3,23},{4,16},{5,17},{6,18},{7,19},{8,28},{9,... | collective-permute-start | bytes 776 | tf_op jit(solution)/shard_map/ppermute | solution.py:449
  11.6 3.5 %copy-start = (bf16[1,1,16,32,128]{4,3,2,1,0:T(8,128)(2,1)S(1)}, bf16[1,1,16,32,128]{4,3,2,1,0:T(8,128)(2,1)}, u32[]{:S(2)}) copy-start(bf16[1,1,16,32,128]{4,3,2,1,0:T(8,128)(2,1)} %param.6) | copy-start | bytes 393220
  11.6 3.5 %copy-start.1 = (f32[1,1,16,4]{2,3,1,0:T(4,128)S(1)}, f32[1,1,16,4]{2,3,1,0:T(4,128)}, u32[]{:S(2)}) copy-start(f32[1,1,16,4]{2,3,1,0:T(4,128)} %param.7) | copy-start | bytes 772
  13.5 31.1 %collective-permute-start.7 = (bf16[1040,128]{1,0:T(8,128)(2,1)S(1)}, bf16[1040,128]{1,0:T(8,128)(2,1)S(1)}, u32[]{:S(2)}, u32[]{:S(2)}) collective-permute-start(bf16[1040,128]{1,0:T(8,128)(2,1)S(1)} %get-tuple-element.23.refs_3_.refs_5_), channel_id=1, source_target_pairs={{0,4},{1,5},{2,6},{3,7},{4,0},{5,1},{6,2},{7,3},{8,12},{9,13},{10,... | collective-permute-start | bytes 798728 | tf_op jit(solution)/shard_map/ppermute | solution.py:440
  15.7 4.0 %collective-permute-start.3 = (bf16[1,272,128]{2,1,0:T(8,128)(2,1)S(1)}, bf16[1,272,128]{2,1,0:T(8,128)(2,1)S(1)}, u32[]{:S(2)}, u32[]{:S(2)}) collective-permute-start(bf16[1,272,128]{2,1,0:T(8,128)(2,1)S(1)} %get-tuple-element.25), channel_id=1, source_target_pairs={{0,1},{1,0},{2,3},{3,2},{4,5},{5,4},{6,7},{7,6},{8,9},{9,8},{10,11... | collective-permute-start | bytes 208904 | tf_op jit(solution)/shard_map/ppermute | solution.py:440
  17.6 41.2 %collective-permute-start.13 = (bf16[1040,128]{1,0:T(8,128)(2,1)S(1)}, bf16[1040,128]{1,0:T(8,128)(2,1)S(1)}, u32[]{:S(2)}, u32[]{:S(2)}) collective-permute-start(bf16[1040,128]{1,0:T(8,128)(2,1)S(1)} %get-tuple-element.28.refs_6_), channel_id=1, source_target_pairs={{0,2},{1,3},{2,4},{3,5},{4,6},{5,7},{6,0},{7,1},{8,10},{9,11},{10,... | collective-permute-start | bytes 798728 | tf_op jit(solution)/shard_map/ppermute | solution.py:440
  19.7 1.5 %copy-start.2 = (s32[1,1,16,4]{2,3,1,0:T(4,128)S(1)}, s32[1,1,16,4]{2,3,1,0:T(4,128)}, u32[]{:S(2)}) copy-start(s32[1,1,16,4]{2,3,1,0:T(4,128)} %param.8) | copy-start | bytes 772
  19.7 8.3 %collective-permute-start.4 = (bf16[2,272,128]{2,1,0:T(8,128)(2,1)S(1)}, bf16[2,272,128]{2,1,0:T(8,128)(2,1)S(1)}, u32[]{:S(2)}, u32[]{:S(2)}) collective-permute-start(bf16[2,272,128]{2,1,0:T(8,128)(2,1)S(1)} %join.3.refs_0_.refs_1_), channel_id=1, source_target_pairs={{0,8},{8,0},{16,24},{24,16},{1,9},{9,1},{17,25},{25,17},{2,10},{10... | collective-permute-start | bytes 417800 | tf_op jit(solution)/shard_map/ppermute | solution.py:468
  25.4 23.8 %collective-permute-start.6 = (bf16[1040,128]{1,0:T(8,128)(2,1)S(1)}, bf16[1040,128]{1,0:T(8,128)(2,1)S(1)}, u32[]{:S(2)}, u32[]{:S(2)}) collective-permute-start(bf16[1040,128]{1,0:T(8,128)(2,1)S(1)} %get-tuple-element.26), channel_id=1, source_target_pairs={{0,5},{1,4},{2,7},{3,6},{4,1},{5,0},{6,3},{7,2},{8,13},{9,12},{10,... | collective-permute-start | bytes 798728 | tf_op jit(solution)/shard_map/ppermute | solution.py:440
  25.9 35.2 %collective-permute-start.12 = (bf16[1040,128]{1,0:T(8,128)(2,1)S(1)}, bf16[1040,128]{1,0:T(8,128)(2,1)S(1)}, u32[]{:S(2)}, u32[]{:S(2)}) collective-permute-start(bf16[1040,128]{1,0:T(8,128)(2,1)S(1)} %get-tuple-element.36), channel_id=1, source_target_pairs={{0,3},{1,2},{2,5},{3,4},{4,7},{5,6},{6,1},{7,0},{8,11},{9,10},{10,... | collective-permute-start | bytes 798728 | tf_op jit(solution)/shard_map/ppermute | solution.py:440
  28.0 1.5 %collective-permute-start.8 = (bf16[1040,128]{1,0:T(8,128)(2,1)S(1)}, bf16[1040,128]{1,0:T(8,128)(2,1)S(1)}, u32[]{:S(2)}, u32[]{:S(2)}) collective-permute-start(bf16[1040,128]{1,0:T(8,128)(2,1)S(1)} %get-tuple-element.29), channel_id=1, source_target_pairs={{0,1},{1,0},{2,3},{3,2},{4,5},{5,4},{6,7},{7,6},{8,9},{9,8},{10,11... | collective-permute-start | bytes 798728 | tf_op jit(solution)/shard_map/ppermute | solution.py:440
  29.6 8.7 %collective-permute-start.5 = (bf16[4,272,128]{2,1,0:T(8,128)(2,1)S(1)}, bf16[4,272,128]{2,1,0:T(8,128)(2,1)S(1)}, u32[]{:S(2)}, u32[]{:S(2)}) collective-permute-start(bf16[4,272,128]{2,1,0:T(8,128)(2,1)S(1)} %join.4.refs_0_), channel_id=1, source_target_pairs={{0,16},{8,24},{16,0},{24,8},{1,17},{9,25},{17,1},{25,9},{2,18},{10... | collective-permute-start | bytes 835592 | tf_op jit(solution)/shard_map/ppermute | solution.py:468
  38.3 25.1 %collective-permute-start.11 = (bf16[1040,128]{1,0:T(8,128)(2,1)S(1)}, bf16[1040,128]{1,0:T(8,128)(2,1)S(1)}, u32[]{:S(2)}, u32[]{:S(2)}) collective-permute-start(bf16[1040,128]{1,0:T(8,128)(2,1)S(1)} %get-tuple-element.32.refs_8_), channel_id=1, source_target_pairs={{0,6},{1,7},{2,0},{3,1},{4,2},{5,3},{6,4},{7,5},{8,14},{9,15},{10,... | collective-permute-start | bytes 798728 | tf_op jit(solution)/shard_map/ppermute | solution.py:440
  47.1 18.5 %collective-permute-start.10 = (bf16[784,128]{1,0:T(8,128)(2,1)S(1)}, bf16[784,128]{1,0:T(8,128)(2,1)S(1)}, u32[]{:S(2)}, u32[]{:S(2)}) collective-permute-start(bf16[784,128]{1,0:T(8,128)(2,1)S(1)} %get-tuple-element.34.refs_8_), channel_id=1, source_target_pairs={{0,7},{1,6},{2,1},{3,0},{4,3},{5,2},{6,5},{7,4},{8,15},{9,14},{10,... | collective-permute-start | bytes 602120 | tf_op jit(solution)/shard_map/ppermute | solution.py:440
  51.8 18.6 %collective-permute-start.9 = (bf16[272,128]{1,0:T(8,128)(2,1)S(1)}, bf16[272,128]{1,0:T(8,128)(2,1)S(1)}, u32[]{:S(2)}, u32[]{:S(2)}) collective-permute-start(bf16[272,128]{1,0:T(8,128)(2,1)S(1)} %get-tuple-element.35), channel_id=1, source_target_pairs={{0,7},{1,6},{2,1},{3,0},{4,3},{5,2},{6,5},{7,4},{8,15},{9,14},{10,... | collective-permute-start | bytes 208904 | tf_op jit(solution)/shard_map/ppermute | solution.py:440

commit v2 on v1

--- a/solution.py
+++ b/solution.py
@@ -99,7 +99,7 @@
 
     def start(self):
         z, refs = self.z, self.refs
-        cols, b = refs[self.cols + "_s"], refs["b"]
+        cols, b = refs[self.cols[0] + "_s"].at[self.cols[1]], refs["b"]
         base = (refs["info"][0] ^ self.flip) * z.half
         first, last = self.rows
 
@@ -114,7 +114,7 @@
 
     def finish(self):
         z, refs = self.z, self.refs
-        table, cols = refs["table"], refs[self.cols + "_v"][...]
+        table, cols = refs["table"], refs[self.cols[0] + "_v"][self.cols[1]]
         kw = table.shape[1]
         both = [entries(cols, h * z.half, z.half, z.rb) for h in range(2)]
         odd = (refs["info"][0] ^ self.flip) == 1
@@ -177,7 +177,7 @@
             rows = pl.ds((i - first) * z.wide, z.wide)
             refs["prod"][rows, :] = jnp.dot(left, b[rows, :], preferred_element_type=F32)
 
-    def finish(self):
+    def finish(self, writer=None):
         z, refs = self.z, self.refs
         first, last = self.rows
         acc, prod, scl_s, col_s = refs["acc"], refs["prod"], refs["scl_s"], refs["col_s"]
@@ -199,6 +199,39 @@
                     placed.append((column // per, moved))
                 for tile, moved in placed:
                     acc[i, tile] = acc[i, tile] + moved
+            if writer is not None:
+                writer.row(i)
+        if writer is not None:
+            writer.finish()
+
+
+class Writer:
+    def __init__(self, sizes, refs):
+        self.z, self.refs, self.sent = sizes, refs, []
+
+    def send(self, at):
+        stage, (i, chunk) = self.refs["stage"], self.sent[at]
+        slot = at % stage.shape[0]
+        width = stage.shape[2]
+        there = self.refs["out"].at[i, :, pl.ds(chunk * width, width)]
+        return pltpu.make_async_copy(stage.at[slot], there, self.refs["out_sems"].at[slot])
+
+    def row(self, i):
+        acc, stage = self.refs["acc"], self.refs["stage"]
+        slots, tiles = stage.shape[0], self.z.tiles // CHUNKS
+        for chunk in range(CHUNKS):
+            at = len(self.sent)
+            if at >= slots:
+                self.send(at - slots).wait()
+            for tile in range(tiles):
+                piece = acc[i, chunk * tiles + tile].astype(BF16)
+                stage[at % slots, :, pl.ds(tile * LANES, LANES)] = piece
+            self.sent.append((i, chunk))
+            self.send(at).start()
+
+    def finish(self):
+        for at in range(max(0, len(self.sent) - self.refs["stage"].shape[0]), len(self.sent)):
+            self.send(at).wait()
 
 
 def clear(acc):
@@ -211,33 +244,13 @@
         lax.fori_loop(0, acc.shape[1], clear_tile, 0, unroll=8)
 
 
-def write_out(sizes, refs, rows):
-    acc, stage, sems, out = refs["acc"], refs["stage"], refs["out_sems"], refs["out"]
-    slots = stage.shape[0]
-    tiles = sizes.tiles // CHUNKS
-    pieces = [(i, chunk) for i in range(*rows) for chunk in range(CHUNKS)]
-
-    def send(at):
-        i, chunk = pieces[at]
-        columns = pl.ds(chunk * tiles * LANES, tiles * LANES)
-        return pltpu.make_async_copy(stage.at[at % slots], out.at[i, :, columns], sems.at[at % slots])
-
-    for at, (i, chunk) in enumerate(pieces):
-        if at >= slots:
-            send(at - slots).wait()
-        for tile in range(tiles):
-            stage[at % slots, :, pl.ds(tile * LANES, LANES)] = acc[i, chunk * tiles + tile].astype(BF16)
-        send(at).start()
-    for at in range(max(0, len(pieces) - slots), len(pieces)):
-        send(at).wait()
-
-
-def first_answers(z, info, cols, b_scl, b_pos, b, rows, after):
+def first_answers(z, info, own_cols, cols, b_scl, b_pos, b, rows):
     rb, kw = b_scl.shape
 
     def body(refs):
         answers = [
-            Gather(z, refs, f"message{flip}", flip, rows, "cols", refs["sems"].at[flip]) for flip in range(2)
+            Gather(z, refs, f"message{flip}", flip, rows, ("cols", 0), refs["sems"].at[flip])
+            for flip in range(2)
         ]
         moves = [
             pltpu.make_async_copy(refs["b_scl"], refs["scl"], refs["sems"].at[2]),
@@ -247,6 +260,8 @@
             move.start()
         for answer in answers:
             answer.start()
+        refs["both"][pl.ds(0, 1)] = refs["own_v"][...]
+        refs["both"][pl.ds(1, 1)] = refs["cols_v"][...]
         for move in moves:
             move.wait()
         scale, column = refs["scl"][...], refs["pos"][...]
@@ -260,11 +275,11 @@
         "info": (info, "smem"),
         "cols_s": (cols, "smem"),
         "cols_v": (cols, "vmem"),
+        "own_v": (own_cols, "vmem"),
         "b_scl": (b_scl, "hbm"),
         "b_pos": (b_pos, "hbm"),
         "b": (b, "hbm"),
     }
-    ins.update({f"after{at}": (array, "any") for at, array in enumerate(after)})
     return kernel_call(
         "first_answers",
         body,
@@ -273,6 +288,7 @@
             "table": pltpu.VMEM((-(-PARTS * rb // 16) * 16, kw), BF16),
             "message0": z.message(rows),
             "message1": z.message(rows),
+            "both": pltpu.VMEM((2,) + cols.shape[1:], I32),
         },
         scratch={
             "scl": pltpu.VMEM(b_scl.shape, F32),
@@ -309,14 +325,15 @@
         refs["both"][pl.ds(0, count)] = refs["own"][...]
         refs["both"][pl.ds(count, count)] = refs["taken"][...]
 
-    outs = {"both": pltpu.VMEM((2 * count,) + own.shape[1:], BF16)}
+    outs = {"both": pltpu.VMEM((2 * count,) + own.shape[1:], own.dtype)}
     return kernel_call("join", body, {"own": (own, "vmem"), "taken": (taken, "vmem")}, outs)["both"]
 
 
-def more_answers(z, info, cols, table, b, rows, after):
+def more_answers(z, info, cols, which, table, b, rows, after):
     def body(refs):
         answers = [
-            Gather(z, refs, f"message{flip}", flip, rows, "cols", refs["sems"].at[flip]) for flip in range(2)
+            Gather(z, refs, f"message{flip}", flip, rows, ("cols", which), refs["sems"].at[flip])
+            for flip in range(2)
         ]
         for answer in answers:
             answer.start()
@@ -341,8 +358,8 @@
 
 def own_blocks(z, info, cols, table, b, rows, kept, after):
     def body(refs):
-        answer = Gather(z, refs, "message", 1, rows, "cols", refs["sems"].at[0])
-        local = Gather(z, refs, "local", 0, rows, "cols", refs["sems"].at[1])
+        answer = Gather(z, refs, "message", 1, rows, ("cols", 0), refs["sems"].at[0])
+        local = Gather(z, refs, "local", 0, rows, ("cols", 0), refs["sems"].at[1])
         local.start()
         answer.start()
         clear(refs["acc"])
@@ -386,7 +403,7 @@
     if answers:
         ins.update(table=(table, "vmem"), b=(b, "hbm"))
         scratch["sems"] = pltpu.SemaphoreType.DMA((len(answers),))
-    for at, (cols, _, span) in enumerate(answers):
+    for at, (cols, _, _, span) in enumerate(answers):
         ins[f"cols{at}_s"] = (cols, "smem")
         ins[f"cols{at}_v"] = (cols, "vmem")
         outs[f"message{at}"] = z.message(span)
@@ -401,8 +418,8 @@
 
     def body(refs):
         gathers = [
-            Gather(z, refs, f"message{at}", side, span, f"cols{at}", refs["sems"].at[at])
-            for at, (_, side, span) in enumerate(answers)
+            Gather(z, refs, f"message{at}", side, span, (f"cols{at}", which), refs["sems"].at[at])
+            for at, (_, which, side, span) in enumerate(answers)
         ]
         for gather in gathers:
             gather.start()
@@ -411,9 +428,7 @@
         add.start()
         for gather in gathers:
             gather.finish()
-        add.finish()
-        if write:
-            write_out(z, refs, rows)
+        add.finish(Writer(z, refs) if write else None)
 
     got = kernel_call("add_message", body, ins, outs, aliases, scratch)
     return got["acc"], [got[f"message{at}"] for at in range(len(answers))], got.get("out")
@@ -439,27 +454,35 @@
         ]
         return lax.ppermute(value, "col", pairs)
 
-    def named_by(by):
+    def named_by(by, cols):
         pairs = []
         for r in range(panels):
             for c in range(columns):
                 to_row = (r + by) % panels
                 to_col = (c - halves * by) % columns
                 pairs.append((r * columns + c, to_row * columns + to_col))
-        return lax.ppermute(a_pos, ("row", "col"), pairs)
-
+        return lax.ppermute(cols, ("row", "col"), pairs)
+
+    every = (0, half)
     order = sorted(range(1, panels), key=lambda by: -min(by, panels - by))
-    every = (0, half)
-    early = (0, half - max(1, half // 4))
-    late = (early[1], half)
     last = order[-1]
-    asked = {by: named_by(by) for by in order}
-
-    got = first_answers(
-        z, info, asked[order[0]], b_scl, b_pos, b_part, every, [asked[by] for by in order[1:]]
-    )
+    own_cols = a_pos[None]
+
+    cols = named_by(order[0], own_cols)
+    got = first_answers(z, info, own_cols, cols, b_scl, b_pos, b_part, every)
     table = got["table"]
     moving = {(order[0], flip): step(got[f"message{flip}"], order[0], flip) for flip in range(halves)}
+
+    asked, known, by = {0: (own_cols, 0)}, [0, order[0]], panels // 4
+    cols = got["both"]
+    while by:
+        more_cols = named_by(by, cols)
+        asked.update({(to + by) % panels: (more_cols, at) for at, to in enumerate(known)})
+        known += [(to + by) % panels for to in known]
+        by //= 2
+        if by:
+            cols = join(cols, more_cols)
+
     pieces = split(z, info, a_part.reshape(nrows * bs, z.wide), a_scl, got["message0"])
     own_left = join(pieces["kept"], step(pieces["given"], 0, 1))
     left = own_left
@@ -467,32 +490,33 @@
     while bit < panels:
         left = join(left, lax.ppermute(left, "row", [(r, r ^ bit) for r in range(panels)]))
         bit *= 2
-    after = got["message0"]
+
+    mine = own_blocks(z, info, own_cols, table, b_part, every, pieces["kept"], got["message0"])
+    taken = step(mine["message"], 0, 1)
+    after = mine["message"]
     for by in order[1:-1]:
-        got = more_answers(z, info, asked[by], table, b_part, every, after)
+        got = more_answers(z, info, *asked[by], table, b_part, every, after)
         after = got["message0"]
         for flip in range(halves):
             moving[by, flip] = step(got[f"message{flip}"], by, flip)
 
-    mine = own_blocks(z, info, a_pos, table, b_part, every, pieces["kept"], after)
-    taken = step(mine["message"], 0, 1)
     more = {"table": table, "b": b_part}
     acc, answers, _ = add_message(
-        z, info, own_left, 0, 1, taken, every, mine["acc"], [(asked[last], 0, every)], **more
+        z, info, own_left, 0, 1, taken, every, mine["acc"], [(*asked[last], 0, every)],
+        after=[after], **more
     )
     ends = answers
     for by in order[:-1]:
         for flip in range(halves):
-            first = by == order[0]
+            first = by == order[0] and flip == 0
             acc, answers, _ = add_message(
                 z, info, left, by, flip, moving[by, flip], every, acc,
-                [(asked[last], 1, late if flip else early)] if first else [],
+                [(*asked[last], 1, every)] if first else [],
                 after=ends[-1:] if first else [], **(more if first else {}),
             )
             ends += answers
     acc = add_message(z, info, left, last, 0, step(ends[0], last, 0), every, acc)[0]
-    acc, _, out = add_message(z, info, left, last, 1, step(ends[1], last, 1), early, acc, write=True)
-    out = add_message(z, info, left, last, 1, step(ends[2], last, 1), late, acc, write=True, out=out)[2]
+    out = add_message(z, info, left, last, 1, step(ends[1], last, 1), every, acc, write=True)[2]
     return out[None, None]
 
 

time: 73.9 us -> 70.2 us (0.950)
  the two profiles are of different devices: /device:TPU:0 before, /device:TPU:25 now
where the time goes in v2:
time: 70.2 us; the launch traced here: 69.9 us
  Pallas kernels  28.2 us (40%)
  starting transfers between devices  20.3 us (29%)
  waiting for transfers between devices  20.3 us (29%)
  local copies, waits for them, and re-layouts  0.78 us (1%)
    pallas_call x14, Pallas kernels, kernel_call(): pl.pallas_call(kernel, out_shape=list(outs.values()), in_specs=in_specs,...  28.2 us
    ppermute x8, starting transfers between devices, step(): return lax.ppermute(value, 'col', pairs)  15.6 us
    ppermute x8, waiting for transfers between devices, step(): return lax.ppermute(value, 'col', pairs)  13.7 us
    ppermute x2, waiting for transfers between devices, named_by(): return lax.ppermute(cols, ('row', 'col'), pairs)  3.35 us
    ppermute x2, waiting for transfers between devices, on_device(): lax.ppermute(left, 'row', [(r, r ^ bit) for r in range(panels)])  3.22 us
    ppermute x2, starting transfers between devices, on_device(): lax.ppermute(left, 'row', [(r, r ^ bit) for r in range(panels)])  2.58 us
    ppermute x2, starting transfers between devices, named_by(): return lax.ppermute(cols, ('row', 'col'), pairs)  2.16 us
  transfers between devices with their start and end apart: 12, of which 3 were waited for; matrix products, arithmetic and copies ran while one was open for 0% of the time, Pallas kernels for 30%

profile of v2, /device:TPU:25, one launch (start us, length us, event | category | flops | bytes accessed | tf_op | source)
XLA Modules:
  0.0 69.9 jit_solution(4260441893425966649)
XLA Ops:
  0.0 1.0 %collective-permute-start = (s32[1,4,16]{2,1,0:T(4,128)}, s32[1,4,16]{2,1,0:T(4,128)S(1)}, u32[]{:S(2)}, u32[]{:S(2)}) collective-permute-start(s32[1,4,16]{2,1,0:T(4,128)} %bitcast.24), channel_id=1, source_target_pairs={{0,20},{1,21},{2,22},{3,23},{4,16},{5,17},{6,18},{7,19},{8,28},{9,... | collective-permute-start | bytes 776 | tf_op jit(solution)/shard_map/ppermute | solution.py:464
  1.0 0.1 stack.23.refs_0_
  1.1 3.3 %collective-permute-done.refs_1_.refs_2_ = s32[1,4,16]{2,1,0:T(4,128)S(1)} collective-permute-done((s32[1,4,16]{2,1,0:T(4,128)}, s32[1,4,16]{2,1,0:T(4,128)S(1)}, u32[]{:S(2)}, u32[]{:S(2)}) %collective-permute-start) | collective-permute-done | bytes 288 | tf_op jit(solution)/shard_map/ppermute | solution.py:464
  4.4 0.0 copy-start.2
  4.4 0.7 copy-done.2
  5.1 0.0 copy-start
  5.1 0.0 copy-start.1
  5.1 1.9 %first_answers.1 = (bf16[32,1024]{1,0:T(8,128)(2,1)S(1)}, bf16[1040,128]{1,0:T(8,128)(2,1)S(1)}, bf16[1040,128]{1,0:T(8,128)(2,1)S(1)}, s32[2,4,16]{2,1,0:T(4,128)S(1)}) custom-call(s32[5]{0:T(128)S(1)} %stack.23.refs_0_, s32[1,4,16]{2,1,0:T(4,128)S(1)} %collective-permute-done.refs_1_.refs_2_, s32[1,4,16]{2,1,0:T(4,128)S(1)} %collective-permute-done.refs_1_.refs_2_, ...), custom_call_target="tpu_custom_call" | custom-call | flops 20000000000 | bytes 1024 | tf_op jit(solution)/shard_map/first_answers/pallas_call | solution.py:78
  7.0 1.1 %collective-permute-start.6 = (s32[2,4,16]{2,1,0:T(4,128)S(1)}, s32[2,4,16]{2,1,0:T(4,128)S(1)}, u32[]{:S(2)}, u32[]{:S(2)}) collective-permute-start(s32[2,4,16]{2,1,0:T(4,128)S(1)} %get-tuple-element.26), channel_id=1, source_target_pairs={{0,14},{1,15},{2,8},{3,9},{4,10},{5,11},{6,12},{7,13},{8,22},{9,23... | collective-permute-start | bytes 1544 | tf_op jit(solution)/shard_map/ppermute | solution.py:464
  8.2 0.1 collective-permute-start.4
  8.2 0.0 copy-done
  8.2 0.0 copy-done.1
  8.2 0.0 copy-start.3
  8.2 0.6 split.1
  8.9 2.4 %collective-permute-start.1 = (bf16[1,272,128]{2,1,0:T(8,128)(2,1)S(1)}, bf16[1,272,128]{2,1,0:T(8,128)(2,1)S(1)}, u32[]{:S(2)}, u32[]{:S(2)}) collective-permute-start(bf16[1,272,128]{2,1,0:T(8,128)(2,1)S(1)} %get-tuple-element.22), channel_id=1, source_target_pairs={{0,1},{1,0},{2,3},{3,2},{4,5},{5,4},{6,7},{7,6},{8,9},{9,8},{10,11... | collective-permute-start | bytes 208904 | tf_op jit(solution)/shard_map/ppermute | solution.py:455
  11.3 2.3 %collective-permute-start.11 = (bf16[1040,128]{1,0:T(8,128)(2,1)S(1)}, bf16[1040,128]{1,0:T(8,128)(2,1)S(1)}, u32[]{:S(2)}, u32[]{:S(2)}) collective-permute-start(bf16[1040,128]{1,0:T(8,128)(2,1)S(1)} %get-tuple-element.32), channel_id=1, source_target_pairs={{0,5},{1,4},{2,7},{3,6},{4,1},{5,0},{6,3},{7,2},{8,13},{9,12},{10,... | collective-permute-start | bytes 798728 | tf_op jit(solution)/shard_map/ppermute | solution.py:455
  13.6 0.0 copy-done.3
  13.6 4.2 %own_blocks.1 = (f32[8,128,32,128]{3,2,1,0:T(8,128)S(1)}, bf16[1040,128]{1,0:T(8,128)(2,1)S(1)}) custom-call(s32[5]{0:T(128)S(1)} %stack.23.refs_0_, s32[1,4,16]{2,1,0:T(4,128)S(1)} %bitcast.26, s32[1,4,16]{2,1,0:T(4,128)S(1)} %bitcast.27, bf16[32,1024]{1,0:T(8,128)(2,1)S(1)} %get-tuple-element.23.refs_3_.refs_4_, bf16[1024,32,128]{2,1,0:T(8,128)(2,1)} %bitcast.29, ...), custom_call_target="tpu_custom_call" | custom-call | flops 20000000000 | bytes 1024 | tf_op jit(solution)/shard_map/own_blocks/pallas_call | solution.py:78
  17.9 0.5 collective-permute-start.5
  18.4 0.0 collective-permute-done.1.refs_1_
  18.4 1.3 %collective-permute-start.2 = (bf16[2,272,128]{2,1,0:T(8,128)(2,1)S(1)}, bf16[2,272,128]{2,1,0:T(8,128)(2,1)S(1)}, u32[]{:S(2)}, u32[]{:S(2)}) collective-permute-start(bf16[2,272,128]{2,1,0:T(8,128)(2,1)S(1)} %join.3.refs_0_.refs_1_), channel_id=1, source_target_pairs={{0,8},{8,0},{16,24},{24,16},{1,9},{9,1},{17,25},{25,17},{2,10},{10... | collective-permute-start | bytes 417800 | tf_op jit(solution)/shard_map/ppermute | solution.py:491
  19.7 0.0 collective-permute-done.6.refs_1_.refs_2_.refs_6_.refs_7_
  19.7 1.9 %more_answers.1 = (bf16[1040,128]{1,0:T(8,128)(2,1)S(1)}, bf16[1040,128]{1,0:T(8,128)(2,1)S(1)}) custom-call(s32[5]{0:T(128)S(1)} %stack.23.refs_0_, s32[2,4,16]{2,1,0:T(4,128)S(1)} %collective-permute-done.6.refs_1_.refs_2_.refs_6_.refs_7_, s32[2,4,16]{2,1,0:T(4,128)S(1)} %collective-permute-done.6.refs_1_.refs_2_.refs_6_.refs_7_, ...), custom_call_target="tpu_custom_call" | custom-call | flops 20000000000 | bytes 1024 | tf_op jit(solution)/shard_map/more_answers/pallas_call | solution.py:78
  21.5 3.4 %collective-permute-start.9 = (bf16[1040,128]{1,0:T(8,128)(2,1)S(1)}, bf16[1040,128]{1,0:T(8,128)(2,1)S(1)}, u32[]{:S(2)}, u32[]{:S(2)}) collective-permute-start(bf16[1040,128]{1,0:T(8,128)(2,1)S(1)} %get-tuple-element.31), channel_id=1, source_target_pairs={{0,3},{1,2},{2,5},{3,4},{4,7},{5,6},{6,1},{7,0},{8,11},{9,10},{10,... | collective-permute-start | bytes 798728 | tf_op jit(solution)/shard_map/ppermute | solution.py:455
  24.9 0.0 collective-permute-done.2.refs_1_
  24.9 1.9 %collective-permute-start.10 = (bf16[1040,128]{1,0:T(8,128)(2,1)S(1)}, bf16[1040,128]{1,0:T(8,128)(2,1)S(1)}, u32[]{:S(2)}, u32[]{:S(2)}) collective-permute-start(bf16[1040,128]{1,0:T(8,128)(2,1)S(1)} %get-tuple-element.27.refs_8_), channel_id=1, source_target_pairs={{0,2},{1,3},{2,4},{3,5},{4,6},{5,7},{6,0},{7,1},{8,10},{9,11},{10,... | collective-permute-start | bytes 798728 | tf_op jit(solution)/shard_map/ppermute | solution.py:455
  26.8 0.0 collective-permute-done.5.refs_2_
  26.8 1.3 %collective-permute-start.3 = (bf16[4,272,128]{2,1,0:T(8,128)(2,1)S(1)}, bf16[4,272,128]{2,1,0:T(8,128)(2,1)S(1)}, u32[]{:S(2)}, u32[]{:S(2)}) collective-permute-start(bf16[4,272,128]{2,1,0:T(8,128)(2,1)S(1)} %join.4.refs_0_), channel_id=1, source_target_pairs={{0,16},{8,24},{16,0},{24,8},{1,17},{9,25},{17,1},{25,9},{2,18},{10... | collective-permute-start | bytes 835592 | tf_op jit(solution)/shard_map/ppermute | solution.py:491
  28.1 2.6 %add_message.7 = (f32[8,128,32,128]{3,2,1,0:T(8,128)S(1)}, bf16[1040,128]{1,0:T(8,128)(2,1)S(1)}) custom-call(s32[5]{0:T(128)S(1)} %stack.23.refs_0_, bf16[2,272,128]{2,1,0:T(8,128)(2,1)S(1)} %join.3.refs_0_.refs_1_, bf16[1040,128]{1,0:T(8,128)(2,1)S(1)} %collective-permute-done.5.refs_2_, ...), custom_call_target="tpu_custom_call", output_to_operand_aliasing={{0}: (3, {})} | custom-call | flops 20000000000 | bytes 1024 | tf_op jit(solution)/shard_map/add_message/pallas_call | solution.py:78
  30.7 3.2 %collective-permute-done.3.refs_1_ = bf16[4,272,128]{2,1,0:T(8,128)(2,1)S(1)} collective-permute-done((bf16[4,272,128]{2,1,0:T(8,128)(2,1)S(1)}, bf16[4,272,128]{2,1,0:T(8,128)(2,1)S(1)}, u32[]{:S(2)}, u32[]{:S(2)}) %collective-permute-start.3) | collective-permute-done | bytes 278560 | tf_op jit(solution)/shard_map/ppermute | solution.py:491
  33.9 0.4 collective-permute-start.8
  34.3 0.0 collective-permute-done.4.refs_2_
  34.3 2.6 %add_message.8 = (f32[8,128,32,128]{3,2,1,0:T(8,128)S(1)}, bf16[1040,128]{1,0:T(8,128)(2,1)S(1)}) custom-call(s32[5]{0:T(128)S(1)} %stack.23.refs_0_, bf16[8,272,128]{2,1,0:T(8,128)(2,1)S(1)} %join.5.refs_1_, bf16[1040,128]{1,0:T(8,128)(2,1)S(1)} %collective-permute-done.4.refs_2_, ...), custom_call_target="tpu_custom_call", output_to_operand_aliasing={{0}: (3, {})} | custom-call | flops 20000000000 | bytes 1024 | tf_op jit(solution)/shard_map/add_message/pallas_call | solution.py:78
  36.9 4.7 %collective-permute-start.7 = (bf16[1040,128]{1,0:T(8,128)(2,1)S(1)}, bf16[1040,128]{1,0:T(8,128)(2,1)S(1)}, u32[]{:S(2)}, u32[]{:S(2)}) collective-permute-start(bf16[1040,128]{1,0:T(8,128)(2,1)S(1)} %get-tuple-element.30), channel_id=1, source_target_pairs={{0,7},{1,6},{2,1},{3,0},{4,3},{5,2},{6,5},{7,4},{8,15},{9,14},{10,... | collective-permute-start | bytes 798728 | tf_op jit(solution)/shard_map/ppermute | solution.py:455
  41.6 0.0 collective-permute-done.11.refs_2_
  41.6 2.2 %add_message.9.refs_3_ = f32[8,128,32,128]{3,2,1,0:T(8,128)S(1)} custom-call(s32[5]{0:T(128)S(1)} %stack.23.refs_0_, bf16[8,272,128]{2,1,0:T(8,128)(2,1)S(1)} %join.5.refs_1_, bf16[1040,128]{1,0:T(8,128)(2,1)S(1)} %collective-permute-done.11.refs_2_, f32[8,128,32,128]{3,2,1,0:T(8,128)S(1)} %get-tuple-element.33.refs_3_), custom_call_target="tpu_custom_call", output_to_operand_aliasing={{}: (3, {})} | custom-call | flops 20000000000 | bytes 1024 | tf_op jit(solution)/shard_map/add_message/pallas_call | solution.py:78
  43.8 13.7 %collective-permute-done.10.refs_2_ = bf16[1040,128]{1,0:T(8,128)(2,1)S(1)} collective-permute-done((bf16[1040,128]{1,0:T(8,128)(2,1)S(1)}, bf16[1040,128]{1,0:T(8,128)(2,1)S(1)}, u32[]{:S(2)}, u32[]{:S(2)}) %collective-permute-start.10) | collective-permute-done | bytes 266272 | tf_op jit(solution)/shard_map/ppermute | solution.py:455
  57.5 2.2 %add_message.10.refs_3_ = f32[8,128,32,128]{3,2,1,0:T(8,128)S(1)} custom-call(s32[5]{0:T(128)S(1)} %stack.23.refs_0_, bf16[8,272,128]{2,1,0:T(8,128)(2,1)S(1)} %join.5.refs_1_, bf16[1040,128]{1,0:T(8,128)(2,1)S(1)} %collective-permute-done.10.refs_2_, f32[8,128,32,128]{3,2,1,0:T(8,128)S(1)} %add_message.9.refs_3_), custom_call_target="tpu_custom_call", output_to_operand_aliasing={{}: (3, {})} | custom-call | flops 20000000000 | bytes 1024 | tf_op jit(solution)/shard_map/add_message/pallas_call | solution.py:78
  59.7 0.0 collective-permute-done.9.refs_2_
  59.7 2.2 %add_message.11.refs_3_ = f32[8,128,32,128]{3,2,1,0:T(8,128)S(1)} custom-call(s32[5]{0:T(128)S(1)} %stack.23.refs_0_, bf16[8,272,128]{2,1,0:T(8,128)(2,1)S(1)} %join.5.refs_1_, bf16[1040,128]{1,0:T(8,128)(2,1)S(1)} %collective-permute-done.9.refs_2_, f32[8,128,32,128]{3,2,1,0:T(8,128)S(1)} %add_message.10.refs_3_), custom_call_target="tpu_custom_call", output_to_operand_aliasing={{}: (3, {})} | custom-call | flops 20000000000 | bytes 1024 | tf_op jit(solution)/shard_map/add_message/pallas_call | solution.py:78
  61.9 0.0 collective-permute-done.8.refs_2_
  62.0 2.2 %add_message.12.refs_3_ = f32[8,128,32,128]{3,2,1,0:T(8,128)S(1)} custom-call(s32[5]{0:T(128)S(1)} %stack.23.refs_0_, bf16[8,272,128]{2,1,0:T(8,128)(2,1)S(1)} %join.5.refs_1_, bf16[1040,128]{1,0:T(8,128)(2,1)S(1)} %collective-permute-done.8.refs_2_, f32[8,128,32,128]{3,2,1,0:T(8,128)S(1)} %add_message.11.refs_3_), custom_call_target="tpu_custom_call", output_to_operand_aliasing={{}: (3, {})} | custom-call | flops 20000000000 | bytes 1024 | tf_op jit(solution)/shard_map/add_message/pallas_call | solution.py:78
  64.2 0.0 collective-permute-done.7.refs_2_
  64.2 5.5 %add_message.13 = (f32[8,128,32,128]{3,2,1,0:T(8,128)S(1)}, bf16[8,32,16384]{2,1,0:T(8,128)(2,1)}) custom-call(s32[5]{0:T(128)S(1)} %stack.23.refs_0_, bf16[8,272,128]{2,1,0:T(8,128)(2,1)S(1)} %join.5.refs_1_, bf16[1040,128]{1,0:T(8,128)(2,1)S(1)} %collective-permute-done.7.refs_2_, ...), custom_call_target="tpu_custom_call", output_to_operand_aliasing={{0}: (3, {})} | custom-call | flops 20000000000 | bytes 1024 | tf_op jit(solution)/shard_map/add_message/pallas_call | solution.py:78
  (3 shorter events, 0.1 us)
Async XLA Ops:
  0.0 4.4 %collective-permute-start = (s32[1,4,16]{2,1,0:T(4,128)}, s32[1,4,16]{2,1,0:T(4,128)S(1)}, u32[]{:S(2)}, u32[]{:S(2)}) collective-permute-start(s32[1,4,16]{2,1,0:T(4,128)} %bitcast.24), channel_id=1, source_target_pairs={{0,20},{1,21},{2,22},{3,23},{4,16},{5,17},{6,18},{7,19},{8,28},{9,... | collective-permute-start | bytes 776 | tf_op jit(solution)/shard_map/ppermute | solution.py:464
  4.4 0.7 copy-start.2
  5.1 3.1 %copy-start = (bf16[1,1,16,32,128]{4,3,2,1,0:T(8,128)(2,1)S(1)}, bf16[1,1,16,32,128]{4,3,2,1,0:T(8,128)(2,1)}, u32[]{:S(2)}) copy-start(bf16[1,1,16,32,128]{4,3,2,1,0:T(8,128)(2,1)} %param.6) | copy-start | bytes 393220
  5.1 3.1 %copy-start.1 = (f32[1,1,16,4]{2,3,1,0:T(4,128)S(1)}, f32[1,1,16,4]{2,3,1,0:T(4,128)}, u32[]{:S(2)}) copy-start(f32[1,1,16,4]{2,3,1,0:T(4,128)} %param.7) | copy-start | bytes 772
  7.0 12.6 %collective-permute-start.6 = (s32[2,4,16]{2,1,0:T(4,128)S(1)}, s32[2,4,16]{2,1,0:T(4,128)S(1)}, u32[]{:S(2)}, u32[]{:S(2)}) collective-permute-start(s32[2,4,16]{2,1,0:T(4,128)S(1)} %get-tuple-element.26), channel_id=1, source_target_pairs={{0,14},{1,15},{2,8},{3,9},{4,10},{5,11},{6,12},{7,13},{8,22},{9,23... | collective-permute-start | bytes 1544 | tf_op jit(solution)/shard_map/ppermute | solution.py:464
  8.2 26.1 %collective-permute-start.4 = (bf16[1040,128]{1,0:T(8,128)(2,1)S(1)}, bf16[1040,128]{1,0:T(8,128)(2,1)S(1)}, u32[]{:S(2)}, u32[]{:S(2)}) collective-permute-start(bf16[1040,128]{1,0:T(8,128)(2,1)S(1)} %get-tuple-element.20.refs_3_.refs_6_), channel_id=1, source_target_pairs={{0,4},{1,5},{2,6},{3,7},{4,0},{5,1},{6,2},{7,3},{8,12},{9,13},{10,... | collective-permute-start | bytes 798728 | tf_op jit(solution)/shard_map/ppermute | solution.py:455
  8.2 5.4 %copy-start.3 = (s32[1,1,16,4]{2,3,1,0:T(4,128)S(1)}, s32[1,1,16,4]{2,3,1,0:T(4,128)}, u32[]{:S(2)}) copy-start(s32[1,1,16,4]{2,3,1,0:T(4,128)} %param.8) | copy-start | bytes 772
  8.9 9.5 %collective-permute-start.1 = (bf16[1,272,128]{2,1,0:T(8,128)(2,1)S(1)}, bf16[1,272,128]{2,1,0:T(8,128)(2,1)S(1)}, u32[]{:S(2)}, u32[]{:S(2)}) collective-permute-start(bf16[1,272,128]{2,1,0:T(8,128)(2,1)S(1)} %get-tuple-element.22), channel_id=1, source_target_pairs={{0,1},{1,0},{2,3},{3,2},{4,5},{5,4},{6,7},{7,6},{8,9},{9,8},{10,11... | collective-permute-start | bytes 208904 | tf_op jit(solution)/shard_map/ppermute | solution.py:455
  11.3 30.3 %collective-permute-start.11 = (bf16[1040,128]{1,0:T(8,128)(2,1)S(1)}, bf16[1040,128]{1,0:T(8,128)(2,1)S(1)}, u32[]{:S(2)}, u32[]{:S(2)}) collective-permute-start(bf16[1040,128]{1,0:T(8,128)(2,1)S(1)} %get-tuple-element.32), channel_id=1, source_target_pairs={{0,5},{1,4},{2,7},{3,6},{4,1},{5,0},{6,3},{7,2},{8,13},{9,12},{10,... | collective-permute-start | bytes 798728 | tf_op jit(solution)/shard_map/ppermute | solution.py:455
  17.9 8.9 %collective-permute-start.5 = (bf16[1040,128]{1,0:T(8,128)(2,1)S(1)}, bf16[1040,128]{1,0:T(8,128)(2,1)S(1)}, u32[]{:S(2)}, u32[]{:S(2)}) collective-permute-start(bf16[1040,128]{1,0:T(8,128)(2,1)S(1)} %get-tuple-element.24.refs_5_), channel_id=1, source_target_pairs={{0,1},{1,0},{2,3},{3,2},{4,5},{5,4},{6,7},{7,6},{8,9},{9,8},{10,11... | collective-permute-start | bytes 798728 | tf_op jit(solution)/shard_map/ppermute | solution.py:455
  18.4 6.5 %collective-permute-start.2 = (bf16[2,272,128]{2,1,0:T(8,128)(2,1)S(1)}, bf16[2,272,128]{2,1,0:T(8,128)(2,1)S(1)}, u32[]{:S(2)}, u32[]{:S(2)}) collective-permute-start(bf16[2,272,128]{2,1,0:T(8,128)(2,1)S(1)} %join.3.refs_0_.refs_1_), channel_id=1, source_target_pairs={{0,8},{8,0},{16,24},{24,16},{1,9},{9,1},{17,25},{25,17},{2,10},{10... | collective-permute-start | bytes 417800 | tf_op jit(solution)/shard_map/ppermute | solution.py:491
  21.5 38.2 %collective-permute-start.9 = (bf16[1040,128]{1,0:T(8,128)(2,1)S(1)}, bf16[1040,128]{1,0:T(8,128)(2,1)S(1)}, u32[]{:S(2)}, u32[]{:S(2)}) collective-permute-start(bf16[1040,128]{1,0:T(8,128)(2,1)S(1)} %get-tuple-element.31), channel_id=1, source_target_pairs={{0,3},{1,2},{2,5},{3,4},{4,7},{5,6},{6,1},{7,0},{8,11},{9,10},{10,... | collective-permute-start | bytes 798728 | tf_op jit(solution)/shard_map/ppermute | solution.py:455
  24.9 32.6 %collective-permute-start.10 = (bf16[1040,128]{1,0:T(8,128)(2,1)S(1)}, bf16[1040,128]{1,0:T(8,128)(2,1)S(1)}, u32[]{:S(2)}, u32[]{:S(2)}) collective-permute-start(bf16[1040,128]{1,0:T(8,128)(2,1)S(1)} %get-tuple-element.27.refs_8_), channel_id=1, source_target_pairs={{0,2},{1,3},{2,4},{3,5},{4,6},{5,7},{6,0},{7,1},{8,10},{9,11},{10,... | collective-permute-start | bytes 798728 | tf_op jit(solution)/shard_map/ppermute | solution.py:455
  26.8 7.1 %collective-permute-start.3 = (bf16[4,272,128]{2,1,0:T(8,128)(2,1)S(1)}, bf16[4,272,128]{2,1,0:T(8,128)(2,1)S(1)}, u32[]{:S(2)}, u32[]{:S(2)}) collective-permute-start(bf16[4,272,128]{2,1,0:T(8,128)(2,1)S(1)} %join.4.refs_0_), channel_id=1, source_target_pairs={{0,16},{8,24},{16,0},{24,8},{1,17},{9,25},{17,1},{25,9},{2,18},{10... | collective-permute-start | bytes 835592 | tf_op jit(solution)/shard_map/ppermute | solution.py:491
  33.9 28.1 %collective-permute-start.8 = (bf16[1040,128]{1,0:T(8,128)(2,1)S(1)}, bf16[1040,128]{1,0:T(8,128)(2,1)S(1)}, u32[]{:S(2)}, u32[]{:S(2)}) collective-permute-start(bf16[1040,128]{1,0:T(8,128)(2,1)S(1)} %get-tuple-element.29.refs_8_), channel_id=1, source_target_pairs={{0,6},{1,7},{2,0},{3,1},{4,2},{5,3},{6,4},{7,5},{8,14},{9,15},{10,... | collective-permute-start | bytes 798728 | tf_op jit(solution)/shard_map/ppermute | solution.py:455
  36.9 27.3 %collective-permute-start.7 = (bf16[1040,128]{1,0:T(8,128)(2,1)S(1)}, bf16[1040,128]{1,0:T(8,128)(2,1)S(1)}, u32[]{:S(2)}, u32[]{:S(2)}) collective-permute-start(bf16[1040,128]{1,0:T(8,128)(2,1)S(1)} %get-tuple-element.30), channel_id=1, source_target_pairs={{0,7},{1,6},{2,1},{3,0},{4,3},{5,2},{6,5},{7,4},{8,15},{9,14},{10,... | collective-permute-start | bytes 798728 | tf_op jit(solution)/shard_map/ppermute | solution.py:455
